TPU v7x, 256 devices: a whole 4x4x8 slice. The times are simulated.
256 devices in a mesh: context: 32 (over x_lo, z, core), tensor: 8 (over y, x_hi).
Axes of the slice: x: 4 (x_hi: 2, x_lo: 2; x = x_hi * 2 + x_lo), y: 4, z: 8, core: 2. Of those that a mesh axis runs over, the one named last changes fastest.
Arguments:
- tokens: bfloat16 [40960, 2048], P(('context', 'tensor')), may hold values from -6 to 6
- w_query: bfloat16 [2048, 2048], P(None, 'tensor'), may hold values from -0.125 to 0.125
- w_key: bfloat16 [2048, 2048], P(None, 'tensor'), may hold values from -0.125 to 0.125
- w_value: bfloat16 [2048, 4096], P(None, 'tensor'), may hold values from -0.125 to 0.125
- w_gate_z: bfloat16 [2048, 4096], P(None, 'tensor'), may hold values from -0.125 to 0.125
- w_gates: bfloat16 [2048, 32, 2], P(None, 'tensor'), may hold values from -0.125 to 0.125
- conv_query: bfloat16 [4, 2048], P(None, 'tensor'), may hold values from -3 to 3
- conv_key: bfloat16 [4, 2048], P(None, 'tensor'), may hold values from -3 to 3
- conv_value: bfloat16 [4, 4096], P(None, 'tensor'), may hold values from -3 to 3
- a_log: float32 [32], P('tensor'), may hold values from -11.52 to 0.7
- dt_bias: float32 [32], P('tensor'), may hold values from -4 to -2
- norm_gain: bfloat16 [128], replicated, may hold values from 0.5 to 1.5
- w_out: bfloat16 [4096, 2048], P('tensor'), may hold values from -0.09375 to 0.09375
Outputs:
- mixed: bfloat16 [40960, 2048], P(('context', 'tensor'))
All inputs are finite; a program needn't handle non-finite values.
Results may differ from a plain program's by a relative error of at most 0.018.
Values may be sent and summed in bfloat16 or wider, within the bound.
A program may use at most 128 MiB of HBM per device.

v0:
```python
import jax
import jax.numpy as jnp
from jax import lax
from jax.sharding import PartitionSpec as P

HK = 16
HV = 32
DK = 128
DV = 128
KW = 4
BLOCK = 64


EPSILON = 1e-06
PRECISE = lax.Precision.HIGHEST


def from_behind(block, axis, distance):
    devices = range(lax.axis_size(axis))
    route = [(i - distance, i) for i in devices if i - distance in devices]
    return lax.ppermute(block, axis, route)


def heads_product(left_term, right_term):
    return jnp.einsum("hij,hjk->hik", left_term, right_term, precision=PRECISE)


def block_product(pattern, left_term, right_term):
    return jnp.einsum(pattern, left_term, right_term, precision=PRECISE)


def unit_rows(channels, head_size):
    shaped = channels.reshape(channels.shape[0], -1, head_size)
    return shaped * lax.rsqrt(jnp.sum(shaped * shaped, axis=-1, keepdims=True) + EPSILON)


def causal_conv(earlier, current, kernel):
    extended = jnp.concatenate([earlier, current], axis=0).astype(jnp.float32)
    weights = kernel.astype(jnp.float32)
    count_rows = current.shape[0]
    summed = weights[0] * extended[0:count_rows]
    for offset in range(1, weights.shape[0]):
        summed = summed + weights[offset] * extended[offset : offset + count_rows]
    return jax.nn.silu(summed)


def to_blocks(array, length):
    return array.reshape(
        array.shape[0] // length, length, array.shape[1], array.shape[2]
    ).transpose(2, 0, 1, 3)


def block_terms(queries, keys, values, decays, strengths, ratio_heads):
    length = keys.shape[2]
    cumulative = jnp.cumsum(decays, axis=-1)
    strict = jnp.tril(jnp.ones((length, length), jnp.float32), -1)
    unit_matrix = jnp.eye(length, dtype=jnp.float32)
    spread = jnp.exp(jnp.minimum(cumulative[..., :, None] - cumulative[..., None, :], 0.0))
    key_key = jnp.repeat(block_product("hbik,hbjk->hbij", keys, keys), ratio_heads, axis=0)
    query_key = jnp.repeat(block_product("hbik,hbjk->hbij", queries, keys), ratio_heads, axis=0)
    keys_wide = jnp.repeat(keys, ratio_heads, axis=0)
    queries_wide = jnp.repeat(queries, ratio_heads, axis=0)
    system = strengths[..., :, None] * spread * strict * key_key + unit_matrix
    growth = jnp.exp(cumulative)
    sources = jnp.concatenate(
        [keys_wide * (strengths * growth)[..., None], values * strengths[..., None]], axis=-1
    )
    solved = jax.scipy.linalg.solve_triangular(system, sources, lower=True, unit_diagonal=True)
    key_size = keys.shape[-1]
    absorb = solved[..., :key_size]
    written = solved[..., key_size:]
    fading = keys_wide * jnp.exp(cumulative[..., -1:] - cumulative)[..., None]
    key_unit = jnp.eye(key_size, dtype=jnp.float32)
    transfer = growth[..., -1][..., None, None] * key_unit - block_product(
        "hbik,hbil->hbkl", fading, absorb
    )
    inject = block_product("hbik,hbiv->hbkv", fading, written)
    reach_map = query_key * spread * (strict + unit_matrix)
    scaled_query = queries_wide * growth[..., None]
    return (scaled_query, reach_map, absorb, written, transfer, inject)


def project_rows(rows_in, w_query, w_key, w_value):
    return tuple(
        (
            jnp.dot(rows_in, matrix, preferred_element_type=jnp.float32).astype(jnp.bfloat16)
            for matrix in (w_query, w_key, w_value)
        )
    )


def per_device(
    tokens,
    w_query,
    w_key,
    w_value,
    w_gate_z,
    w_gates,
    conv_query,
    conv_key,
    conv_value,
    a_log,
    dt_bias,
    norm_gain,
    w_out,
):
    margin = KW - 1
    ratio_heads = HV // HK
    heads_value = w_value.shape[1] // DV
    gathered = lax.all_gather(tokens, "tensor", axis=0, tiled=True)
    count_rows = gathered.shape[0]
    pre_query, pre_key, pre_value = project_rows(gathered, w_query, w_key, w_value)
    earlier = from_behind(
        (
            pre_query[count_rows - margin :],
            pre_key[count_rows - margin :],
            pre_value[count_rows - margin :],
        ),
        "context",
        1,
    )
    gate_z = jnp.dot(gathered, w_gate_z, preferred_element_type=jnp.float32).astype(jnp.bfloat16)
    gate_logits = jnp.dot(
        gathered,
        w_gates.reshape(w_gates.shape[0], 2 * heads_value),
        preferred_element_type=jnp.float32,
    ).astype(jnp.bfloat16)
    pre_query, pre_key, pre_value, gate_z, gate_logits = lax.optimization_barrier(
        (pre_query, pre_key, pre_value, gate_z, gate_logits)
    )
    conv_q = causal_conv(earlier[0], pre_query, conv_query)
    conv_k = causal_conv(earlier[1], pre_key, conv_key)
    conv_v = causal_conv(earlier[2], pre_value, conv_value)
    queries = unit_rows(conv_q, DK) * DK ** (-0.5)
    keys_all = unit_rows(conv_k, DK)
    values_all = conv_v.reshape(count_rows, heads_value, DV)
    logits = gate_logits.astype(jnp.float32).reshape(count_rows, heads_value, 2)
    decays = -jnp.exp(a_log)[None, :] * jax.nn.softplus(logits[..., 0] + dt_bias[None, :])
    strengths = jax.nn.sigmoid(logits[..., 1])
    count_blocks = count_rows // BLOCK
    decay_blocks = decays.reshape(count_blocks, BLOCK, heads_value).transpose(2, 0, 1)
    strength_blocks = strengths.reshape(count_blocks, BLOCK, heads_value).transpose(2, 0, 1)
    terms = block_terms(
        to_blocks(queries, BLOCK),
        to_blocks(keys_all, BLOCK),
        to_blocks(values_all, BLOCK),
        decay_blocks,
        strength_blocks,
        ratio_heads,
    )
    moved = tuple((jnp.moveaxis(array, 1, 0) for array in terms))
    identity = jnp.broadcast_to(jnp.eye(DK, dtype=jnp.float32), (heads_value, DK, DK))
    empty_state = jnp.zeros((heads_value, DK, DV), jnp.float32)

    def compose(totals, items):
        move_b, add_b = items
        return ((heads_product(move_b, totals[0]), heads_product(move_b, totals[1]) + add_b), None)

    (whole_move, whole_add), unused = lax.scan(
        compose, (identity, empty_state), (moved[4], moved[5])
    )

    def relay(turn, incoming):
        return from_behind(
            (heads_product(whole_move, incoming) + whole_add).astype(jnp.bfloat16), "context", 1
        ).astype(jnp.float32)

    entering = lax.fori_loop(0, lax.axis_size("context") - 1, relay, empty_state)

    def advance(current, items):
        query_b, reach_b, absorb_b, written_b, move_b, add_b = items
        fixed = written_b - heads_product(absorb_b, current)
        outputs_b = heads_product(query_b, current) + heads_product(reach_b, fixed)
        return (heads_product(move_b, current) + add_b, outputs_b)

    final_state, core = lax.scan(advance, entering, moved)
    core_rows = core.transpose(0, 2, 1, 3).reshape(count_rows, heads_value, DV)
    gate_values = gate_z.astype(jnp.float32).reshape(count_rows, heads_value, DV)
    mean_square = jnp.mean(core_rows * core_rows, axis=-1, keepdims=True)
    normed = (
        core_rows
        * lax.rsqrt(mean_square + EPSILON)
        * norm_gain.astype(jnp.float32)
        * jax.nn.silu(gate_values)
    )
    normed = normed.reshape(count_rows, heads_value * DV).astype(jnp.bfloat16)
    return lax.psum_scatter(
        jnp.dot(normed, w_out, preferred_element_type=jnp.float32).astype(jnp.bfloat16),
        "tensor",
        scatter_dimension=0,
        tiled=True,
    )


def solution(mesh):
    placed = (
        P(("context", "tensor"), None),
        P(None, "tensor"),
        P(None, "tensor"),
        P(None, "tensor"),
        P(None, "tensor"),
        P(None, "tensor", None),
        P(None, "tensor"),
        P(None, "tensor"),
        P(None, "tensor"),
        P("tensor"),
        P("tensor"),
        P(),
        P("tensor", None),
    )
    return jax.shard_map(
        per_device,
        mesh=mesh,
        in_specs=placed,
        out_specs=P(("context", "tensor"), None),
        check_vma=False,
    )
```

profile of v0, /device:TPU:2, one launch (start us, length us, event | category | flops | bytes accessed | tf_op | source)
XLA Modules:
  0.0 1188.1 jit_solution(1584786257971877445)
XLA Ops:
  17.5 79.7 %all-gather.2.cloned.1.call-done = bf16[1280,2048]{1,0:T(8,128)(2,1)} async-done(((bf16[160,2048]{1,0:T(8,128)(2,1)}), bf16[1280,2048]{1,0:T(8,128)(2,1)}) %all-gather.2.cloned.1.call-update) | async-done | bytes 5242896 | tf_op jit(solution)/shard_map/all_gather | solution.py:110
  97.2 4.5 convolution_convert_fusion.3
  105.3 2.9 convolution_convert_fusion.2
  108.3 4.1 convolution_convert_fusion.1
  115.8 3.6 collective-permute-start.3
  126.2 2.6 maximum_convert_fusion.1
  130.7 3.1 mul.342
  133.8 4.1 reduce_sum.27
  145.4 3.2 fusion.86
  150.9 2.8 mul.384
  153.7 4.1 reduce_sum.28
  161.8 2.8 reshape.216
  172.2 3.0 select_add_fusion
  177.9 394.6 %custom-call.4 = f32[4,20,1,64,64]{3,4,2,1,0:T(8,128)} custom-call(f32[4,20,1,64,64]{4,3,2,1,0:T(8,128)} %select_add_fusion), custom_call_target="InvertDiagBlocksLowerTriangular" | custom-call | tf_op jit(solution)/shard_map/jit(_solve_triangular)/vmap(vmap())/triangular_solve | solution.py:68
  572.5 3.5 bitcast_multiply_fusion
  577.2 3.1 divide_multiply_fusion
  580.3 4.0 reshape_reshape.3
  584.2 11.4 bitcast_multiply_fusion.3
  595.7 5.4 fusion.31
  601.1 3.1 slice_bitcast_fusion.1
  604.2 8.8 fusion.51
  613.0 2.7 copy.97
  615.6 9.3 bitcast_subtract_fusion
  625.0 3.0 copy.96
  628.0 57.2 %while.37 = (s32[]{:T(128)}, f32[4,128,128]{2,1,0:T(8,128)S(1)}, f32[4,128,128]{2,1,0:T(8,128)S(1)}, f32[20,4,128,128]{3,2,1,0:T(8,128)}, f32[20,4,128,128]{3,2,1,0:T(8,128)}, /*index=5*/s32[]{:T(128)}, s32[]{:T(128)}) while((s32[]{:T(128)}, f32[4,128,128]{2,1,0:T(8,128)S(1)}, f32[4,128,128]{2,1,0:T(8,128)S(1)}, ...), condition=%wide.region_3.4_spmd.clone, body=%wide.region_2.3_spmd.clone.sunk | while | flops 201457664 | bytes 2885207 | solution.py:159
  685.2 273.9 %while.38 = (s32[]{:T(128)}, f32[4,128,128]{2,1,0:T(8,128)S(1)}, f32[4,128,128]{2,1,0:T(8,128)S(1)}, f32[4,128,128]{2,1,0:T(8,128)S(1)}, s32[]{:T(128)}, /*index=5*/s32[]{:T(128)}) while((s32[]{:T(128)}, f32[4,128,128]{2,1,0:T(8,128)S(1)}, f32[4,128,128]{2,1,0:T(8,128)S(1)}, f32[4,128,128]{2,1,0:T(8,128)S(1)}, s32[]{:T(128)}, ...), condition=%wide.region_5.6_spmd.clone, body=%wide.region_4.5_spmd.clone.sunk | while | flops 100925440 | bytes 1835127 | solution.py:168
  685.7 3.6 collective-permute-start
  689.2 4.8 collective-permute-done
  696.4 6.5 collective-permute-done
  705.3 6.5 collective-permute-done
  714.1 6.5 collective-permute-done
  722.9 6.5 collective-permute-done
  731.8 6.5 collective-permute-done
  740.6 6.5 collective-permute-done
  749.4 6.5 collective-permute-done
  758.3 6.5 collective-permute-done
  767.1 6.5 collective-permute-done
  776.0 6.5 collective-permute-done
  784.8 6.5 collective-permute-done
  793.6 6.5 collective-permute-done
  802.5 6.5 collective-permute-done
  811.3 6.5 collective-permute-done
  820.1 6.5 collective-permute-done
  829.0 6.5 collective-permute-done
  837.8 6.5 collective-permute-done
  846.7 6.5 collective-permute-done
  855.5 6.5 collective-permute-done
  864.3 6.5 collective-permute-done
  873.2 6.5 collective-permute-done
  882.0 6.5 collective-permute-done
  890.8 6.5 collective-permute-done
  899.7 6.5 collective-permute-done
  908.5 6.5 collective-permute-done
  917.4 6.5 collective-permute-done
  926.2 6.5 collective-permute-done
  935.0 6.5 collective-permute-done
  943.9 6.5 collective-permute-done
  952.7 6.5 collective-permute-done
  959.2 118.3 %while.36 = (s32[]{:T(128)}, f32[4,128,128]{2,1,0:T(8,128)S(1)}, f32[20,4,64,128]{3,2,1,0:T(8,128)}, f32[20,4,128,128]{3,2,1,0:T(8,128)}, f32[20,4,128,128]{3,2,...) while((s32[]{:T(128)}, f32[4,128,128]{2,1,0:T(8,128)S(1)}, ...), condition=%wide.region_8.9_spmd, body=%wide.region_7.8_spmd.sunk | while | flops 226623488 | bytes 3280485 | solution.py:176
  1077.5 2.5 multiply_reduce_fusion
  1080.4 3.7 copy.109
  1084.1 2.9 mul.395
  1087.0 4.9 convolution_convert_fusion
  1092.0 88.9 %reduce-scatter.2.cloned.1.call-done = bf16[160,2048]{1,0:T(8,128)(2,1)} async-done(((bf16[1280,2048]{1,0:T(8,128)(2,1)}), bf16[160,2048]{1,0:T(8,128)(2,1)}) %reduce-scatter.2.cloned.1.call-update) | async-done | bytes 655376 | tf_op jit(solution)/shard_map/reduce_scatter | solution.py:187
  (414 shorter events, 296.0 us)
Async XLA Ops:
  6.5 1080.5 %copy-start = (bf16[512,2048]{1,0:T(8,128)(2,1)S(1)}, bf16[512,2048]{1,0:T(8,128)(2,1)}, u32[]{:S(2)}) copy-start(bf16[512,2048]{1,0:T(8,128)(2,1)} %param.31) | copy-start | bytes 6291460
  6.5 90.7 %all-gather.2.cloned.1.call-start = ((), (), s32[]{:S(2)}) async-start(), calls=%async_computation.1 | async-start | bytes 5898240 | tf_op jit(solution)/shard_map/all_gather | solution.py:110
  7.3 1173.6 %reduce-scatter.2.cloned.1.call-start = ((), (), s32[]{:S(2)}) async-start(), calls=%async_computation.2 | async-start | bytes 5898240 | tf_op jit(solution)/shard_map/reduce_scatter | solution.py:187
  17.5 84.8 %copy-start.38 = (bf16[2048,256]{1,0:T(8,128)(2,1)S(1)}, bf16[2048,256]{1,0:T(8,128)(2,1)}, u32[]{:S(2)}) copy-start(bf16[2048,256]{1,0:T(8,128)(2,1)} %param.20) | copy-start | bytes 3145732
  97.2 5.1 copy-start.6
  101.7 2.2 copy-start.11
  102.3 3.0 copy-start.36
  105.3 2.9 copy-start.37
  108.3 14.7 %copy-start.9 = (bf16[1280,512]{1,0:T(8,128)(2,1)}, bf16[1280,512]{1,0:T(8,128)(2,1)S(1)}, u32[]{:S(2)}) copy-start(bf16[1280,512]{1,0:T(8,128)(2,1)S(1)} %convolution_convert_fusion.2) | copy-start | bytes 3932164
  113.8 12.3 %collective-permute-start.1 = (bf16[3,256]{1,0:T(4,128)(2,1)}, bf16[3,256]{1,0:T(4,128)(2,1)}, u32[]{:S(2)}, u32[]{:S(2)}) collective-permute-start(bf16[3,256]{1,0:T(4,128)(2,1)} %slice.141), channel_id=1, source_target_pairs={{0,8},{8,16},{16,24},{24,32},{32,40},{40,48},{48,56},{56,64},{64,7... | collective-permute-start | bytes 4616 | tf_op jit(solution)/shard_map/ppermute | solution.py:21
  115.8 10.4 collective-permute-start.3
  121.3 7.5 copy-start.31
  121.3 7.5 copy-start.32
  121.3 7.5 copy-start.33
  121.3 7.5 copy-start.34
  124.2 451.8 %collective-permute-start.2 = (bf16[3,512]{1,0:T(4,128)(2,1)}, bf16[3,512]{1,0:T(4,128)(2,1)}, u32[]{:S(2)}, u32[]{:S(2)}) collective-permute-start(bf16[3,512]{1,0:T(4,128)(2,1)} %slice.152), channel_id=1, source_target_pairs={{0,8},{8,16},{16,24},{24,32},{32,40},{40,48},{48,56},{56,64},{64,7... | collective-permute-start | bytes 9224 | tf_op jit(solution)/shard_map/ppermute | solution.py:21
  145.3 3.3 copy-start.1
  145.3 3.3 copy-start.27
  145.3 3.3 copy-start.28
  145.4 3.2 copy-start.29
  145.4 3.2 copy-start.30
  176.0 396.5 %copy-start.14 = (f32[4,20,64]{2,1,0:T(8,128)S(1)}, f32[4,20,64]{2,1,0:T(8,128)}, u32[]{:S(2)}) copy-start(f32[4,20,64]{2,1,0:T(8,128)} %get-tuple-element.263) | copy-start | bytes 61444
  176.0 396.5 %copy-start.15 = (f32[4,20,64]{2,1,0:T(8,128)S(1)}, f32[4,20,64]{2,1,0:T(8,128)}, u32[]{:S(2)}) copy-start(f32[4,20,64]{2,1,0:T(8,128)} %get-tuple-element.264) | copy-start | bytes 61444
  572.5 3.5 copy-start.10
  584.2 11.4 copy-start.5
  584.2 11.5 copy-start.8
  601.1 3.1 copy-start.4
  612.9 2.7 copy-start.13
  613.0 2.7 copy-start.22
  625.0 3.0 copy-start.3
  628.0 57.2 %copy-start.2 = (f32[4,128,128]{2,1,0:T(8,128)S(1)}, f32[4,128,128]{2,1,0:T(8,128)}, u32[]{:S(2)}) copy-start(f32[4,128,128]{2,1,0:T(8,128)} %custom-call.6) | copy-start | bytes 786436
  685.7 8.4 collective-permute-start
  694.5 8.4 collective-permute-start
  703.3 8.4 collective-permute-start
  712.2 8.4 collective-permute-start
  721.0 8.4 collective-permute-start
  729.8 8.4 collective-permute-start
  738.7 8.4 collective-permute-start
  747.5 8.4 collective-permute-start
  756.4 8.4 collective-permute-start
  765.2 8.4 collective-permute-start
  774.0 8.4 collective-permute-start
  782.9 8.4 collective-permute-start
  791.7 8.4 collective-permute-start
  800.5 8.4 collective-permute-start
  809.4 8.4 collective-permute-start
  818.2 8.4 collective-permute-start
  827.1 8.4 collective-permute-start
  835.9 8.4 collective-permute-start
  844.7 8.4 collective-permute-start
  853.6 8.4 collective-permute-start
  862.4 8.4 collective-permute-start
  871.2 8.4 collective-permute-start
  880.1 8.4 collective-permute-start
  888.9 8.4 collective-permute-start
  897.7 8.4 collective-permute-start
  906.6 8.4 collective-permute-start
  915.4 8.4 collective-permute-start
  924.3 8.4 collective-permute-start
  933.1 8.4 collective-permute-start
  941.9 8.4 collective-permute-start
  950.8 8.4 collective-permute-start
  1084.1 3.0 copy-start.35
  1084.1 3.0 copy-start.39
  (12 other events, 11.9 us)
Sparse Core Ops, SparseCore 0:
  9.9 87.2 all-gather.1
  1092.1 88.7 reduce-scatter.1
where the time goes:
time: 1200 us; the launch traced here: 1190 us
  other arithmetic  453 us (38%)
  waiting for transfers between devices  368 us (31%)
  matrix products  233 us (19%)
  starting transfers between devices  68.6 us (6%)
  local copies, waits for them, and re-layouts  47.7 us (4%)
  between operations  14.4 us (1%)
    another operation x5, other arithmetic, block_terms(): jax.scipy.linalg.solve_triangular(system, sources, lower=True, unit_diago...  399 us
    ppermute x34, waiting for transfers between devices, from_behind(): return lax.ppermute(block, axis, route)  199 us
    dot_general x151, matrix products, heads_product(): return jnp.einsum('hij,hjk->hik', left_term, right_term, precision=PRECISE)  185 us
    reduce_scatter x1, waiting for transfers between devices, per_device(): lax.psum_scatter(jnp.dot(normed, w_out, preferred_element_type=jnp.float3...  88.9 us
    all_gather x1, waiting for transfers between devices, per_device(): gathered = lax.all_gather(tokens, 'tensor', axis=0, tiled=True)  79.7 us
    ppermute x34, starting transfers between devices, from_behind(): return lax.ppermute(block, axis, route)  68.6 us
  transfers between devices with their start and end apart: 36, of which 33 were waited for; matrix products, arithmetic and copies ran while one was open for 39% of the time, Pallas kernels for 0%

commit v1 on v0

v1 whole, which is shorter than its diff:
```python
import functools

import jax
import jax.numpy as jnp
from jax import lax
from jax.experimental import pallas as pl
from jax.experimental.pallas import tpu as pltpu
from jax.sharding import PartitionSpec as P

HK = 16
HV = 32
DK = 128
DV = 128
KW = 4
EPSILON = 1e-06
LEN = 128
PER_STEP = 2
HEADS = 4
KEYS = 2
F32 = jnp.float32
B16 = jnp.bfloat16


def mm(a, b):
    return jnp.dot(a, b, preferred_element_type=F32)


def mm_nt(a, b):
    return lax.dot_general(a, b, (((1,), (1,)), ((), ())), preferred_element_type=F32)


def mm_tn(a, b):
    return lax.dot_general(a, b, (((0,), (0,)), ((), ())), preferred_element_type=F32)


def silu(x):
    return x / (1.0 + jnp.exp(-x))


def unit(x):
    return x * lax.rsqrt(jnp.sum(x * x, axis=-1, keepdims=True) + EPSILON)


def chunk_terms(q_all, k_all, v_all, gates, gate_par):
    ii = lax.broadcasted_iota(jnp.int32, (LEN, LEN), 0)
    jj = lax.broadcasted_iota(jnp.int32, (LEN, LEN), 1)
    lower = (ii >= jj).astype(F32)
    strict = (ii > jj).astype(F32)
    differ = ii ^ jj
    levels = [((differ >> s) == 1).astype(B16) for s in range(LEN.bit_length() - 1)]
    eye = (ii == jj).astype(B16)

    logits = gates.astype(F32)
    shifted = logits + gate_par[1:2, :]
    softplus = jnp.maximum(shifted, 0.0) + jnp.log1p(jnp.exp(-jnp.abs(shifted)))
    decays = -jnp.exp(gate_par[0:1, :]) * softplus
    beta = 1.0 / (1.0 + jnp.exp(-logits))
    cum = jnp.dot(lower, decays, preferred_element_type=F32, precision=lax.Precision.HIGHEST)
    cum_t = cum.T
    growth = jnp.exp(cum)
    fade = jnp.exp(cum[LEN - 1 : LEN, :] - cum)

    terms = []
    for g in range(KEYS):
        qf = unit(q_all[:, g * DK : (g + 1) * DK]) * (DK**-0.5)
        kf = unit(k_all[:, g * DK : (g + 1) * DK])
        qb, kb = qf.astype(B16), kf.astype(B16)
        kk = mm_nt(kb, kb) * strict
        qk = mm_nt(qb, kb) * lower
        for h in (2 * g, 2 * g + 1):
            spread = jnp.exp(jnp.minimum(cum[:, h : h + 1] - cum_t[h : h + 1, :], 0.0))
            b = beta[:, 4 + h : 5 + h]
            a = (kk * spread * b).astype(B16)
            r = (qk * spread).astype(B16)
            vb = (v_all[:, h * DV : (h + 1) * DV] * b).astype(B16)
            grow = growth[:, h : h + 1]
            src = jnp.concatenate([(kf * (b * grow)).astype(B16), vb], axis=1)
            fk = (kf * fade[:, h : h + 1]).astype(B16)
            terms.append([a, r, src, fk, qf * grow, growth[LEN - 1 : LEN, h : h + 1]])
    inv = [eye - t[0] * levels[0] for t in terms]
    for level in levels[1:]:
        part = [mm(t[0] * level, x).astype(B16) for t, x in zip(terms, inv)]
        inv = [x - mm(x, p).astype(B16) for x, p in zip(inv, part)]
    out = []
    for (a, r, src, fk, qg, last), x in zip(terms, inv):
        yw = mm(x, src).astype(B16)
        ryw = mm(r, yw)
        fyw = mm_tn(fk, yw)
        q_new = (qg - ryw[:, :DK]).astype(B16)
        out.append((q_new, ryw[:, DK:], fyw[:, :DK].astype(B16), fyw[:, DK:], last))
    return out


def local_kernel(pre_ref, tail_ref, gates_ref, taps_ref, par_ref, op_ref, os_ref, x_ref, ext):
    step = pl.program_id(0)
    rows = LEN * PER_STEP

    @pl.when(step == 0)
    def _():
        ext[0:8, :] = tail_ref[...].astype(F32)[8:16, :]
        eye = lax.broadcasted_iota(jnp.int32, (DK, 2 * DK), 0) == lax.broadcasted_iota(
            jnp.int32, (DK, 2 * DK), 1
        )
        for h in range(HEADS):
            x_ref[h] = eye.astype(F32)

    @pl.when(step > 0)
    def _():
        ext[0:8, :] = ext[rows : rows + 8, :]

    ext[8 : rows + 8, :] = pre_ref[...].astype(F32)
    taps = taps_ref[...]
    par = par_ref[...]
    done = []
    for c in range(PER_STEP):
        base = c * LEN + 8
        conv = taps[0:1, :] * ext[base - 3 : base - 3 + LEN, :]
        for j in range(1, KW):
            conv = conv + taps[j : j + 1, :] * ext[base - 3 + j : base - 3 + j + LEN, :]
        conv = silu(conv)
        done.append(
            chunk_terms(
                conv[:, :256], conv[:, 256:512], conv[:, 512:], gates_ref[c * LEN : (c + 1) * LEN, :], par
            )
        )
    for h in range(HEADS):
        x = x_ref[h]
        for c in range(PER_STEP):
            q_new, own, move, add, last = done[c][h]
            xb = x.astype(B16)
            seen = mm(q_new, xb)
            at = slice(c * LEN, (c + 1) * LEN)
            cols = slice(h * DV, (h + 1) * DV)
            op_ref[at, cols] = seen[:, :DK].astype(B16)
            os_ref[at, cols] = seen[:, DK:] + own
            x = x * last - mm(move, xb)
            x = jnp.concatenate([x[:, :DK], x[:, DK:] + add], axis=1)
        x_ref[h] = x


def local_pass(pre, tail, gates, taps, par):
    rows = LEN * PER_STEP
    total = pre.shape[0]
    return pl.pallas_call(
        local_kernel,
        grid=(total // rows,),
        in_specs=[
            pl.BlockSpec((rows, 1024), lambda i: (i, 0)),
            pl.BlockSpec((16, 1024), lambda i: (0, 0)),
            pl.BlockSpec((rows, 128), lambda i: (i, 0)),
            pl.BlockSpec((8, 1024), lambda i: (0, 0)),
            pl.BlockSpec((8, 128), lambda i: (0, 0)),
        ],
        out_specs=[
            pl.BlockSpec((rows, 512), lambda i: (i, 0)),
            pl.BlockSpec((rows, 512), lambda i: (i, 0)),
            pl.BlockSpec((HEADS, DK, 2 * DK), lambda i: (0, 0, 0)),
        ],
        out_shape=[
            jax.ShapeDtypeStruct((total, 512), B16),
            jax.ShapeDtypeStruct((total, 512), F32),
            jax.ShapeDtypeStruct((HEADS, DK, 2 * DK), F32),
        ],
        scratch_shapes=[pltpu.VMEM((rows + 8, 1024), F32)],
        compiler_params=pltpu.CompilerParams(
            dimension_semantics=("arbitrary",), vmem_limit_bytes=48 * 1024 * 1024
        ),
    )(pre, tail, gates, taps, par)


def finish_rows(seen, own, z, gain, state):
    parts = []
    for h in range(HEADS):
        cols = slice(h * DV, (h + 1) * DV)
        core = mm(seen[:, cols], state[h]) + own[:, cols]
        scale = lax.rsqrt(jnp.mean(core * core, axis=-1, keepdims=True) + EPSILON)
        parts.append((core * scale * gain * silu(z[:, cols].astype(F32))).astype(B16))
    return jnp.concatenate(parts, axis=1)


def finish_kernel(op_ref, os_ref, z_ref, gain_ref, state_ref, w_ref, out_ref):
    normed = finish_rows(op_ref[...], os_ref[...], z_ref[...], gain_ref[...], state_ref[...])
    out_ref[...] = mm(normed, w_ref[...]).astype(B16)


def finish(op, os, z, gain, state, w_out):
    rows = 160
    total, width = op.shape[0], w_out.shape[1]
    return pl.pallas_call(
        finish_kernel,
        grid=(total // rows,),
        in_specs=[
            pl.BlockSpec((rows, 512), lambda i: (i, 0)),
            pl.BlockSpec((rows, 512), lambda i: (i, 0)),
            pl.BlockSpec((rows, 512), lambda i: (i, 0)),
            pl.BlockSpec((1, DV), lambda i: (0, 0)),
            pl.BlockSpec((HEADS, DK, DV), lambda i: (0, 0, 0)),
            pl.BlockSpec((512, width), lambda i: (0, 0)),
        ],
        out_specs=pl.BlockSpec((rows, width), lambda i: (i, 0)),
        out_shape=jax.ShapeDtypeStruct((total, width), B16),
        compiler_params=pltpu.CompilerParams(
            dimension_semantics=("arbitrary",), vmem_limit_bytes=48 * 1024 * 1024
        ),
    )(op, os, z, gain, state, w_out)


def from_behind(block, axis, distance):
    devices = range(lax.axis_size(axis))
    route = [(i - distance, i) for i in devices if i - distance in devices]
    return lax.ppermute(block, axis, route)


def entering_state(x):
    x = from_behind(x.astype(B16), "context", 1)
    distance, count = 1, lax.axis_size("context")
    while distance < count:
        last = 2 * distance >= count
        sent = x[:, :, DK:] if last else x
        got = from_behind(sent, "context", distance)
        moved = jnp.einsum("hij,hjk->hik", x[:, :, :DK], got, preferred_element_type=F32)
        if last:
            x = moved + x[:, :, DK:].astype(F32)
        else:
            add = jnp.concatenate([jnp.zeros_like(x[:, :, :DK]), x[:, :, DK:]], axis=2)
            x = (moved + add.astype(F32)).astype(B16)
        distance *= 2
    return x.astype(B16)


def gate_weights(w_gates):
    order = w_gates.transpose(0, 2, 1).reshape(w_gates.shape[0], 2 * HEADS)
    return jnp.pad(order, ((0, 0), (0, 128 - 2 * HEADS)))


def small_inputs(conv_query, conv_key, conv_value, a_log, dt_bias, norm_gain):
    taps = jnp.concatenate([conv_query, conv_key, conv_value], axis=1).astype(F32)
    taps = jnp.pad(taps, ((0, 8 - KW), (0, 0)))
    par = jnp.pad(jnp.stack([a_log, dt_bias]), ((0, 6), (0, 128 - HEADS)))
    return taps, par, norm_gain.astype(F32)[None, :]


def per_device(
    tokens,
    w_query,
    w_key,
    w_value,
    w_gate_z,
    w_gates,
    conv_query,
    conv_key,
    conv_value,
    a_log,
    dt_bias,
    norm_gain,
    w_out,
):
    taps, par, gain = small_inputs(conv_query, conv_key, conv_value, a_log, dt_bias, norm_gain)
    gathered = lax.all_gather(tokens, "tensor", axis=0, tiled=True)
    weights = jnp.concatenate([w_query, w_key, w_value], axis=1)
    pre = mm(gathered, weights).astype(B16)
    tail = from_behind(pre[pre.shape[0] - 16 :], "context", 1)
    z = mm(gathered, w_gate_z).astype(B16)
    gates = mm(gathered, gate_weights(w_gates)).astype(B16)
    op, os, x = local_pass(pre, tail, gates, taps, par)
    state = entering_state(x)
    partial = finish(op, os, z, gain, state, w_out)
    return lax.psum_scatter(partial, "tensor", scatter_dimension=0, tiled=True)


def solution(mesh):
    placed = (
        P(("context", "tensor"), None),
        P(None, "tensor"),
        P(None, "tensor"),
        P(None, "tensor"),
        P(None, "tensor"),
        P(None, "tensor", None),
        P(None, "tensor"),
        P(None, "tensor"),
        P(None, "tensor"),
        P("tensor"),
        P("tensor"),
        P(),
        P("tensor", None),
    )
    return jax.shard_map(
        per_device,
        mesh=mesh,
        in_specs=placed,
        out_specs=P(("context", "tensor"), None),
        check_vma=False,
    )
```

time: 1200 us -> 325 us (0.27)
  other arithmetic: 453 us -> 1.44 us
  matrix products: 233 us -> 14.3 us
  waiting for transfers between devices: 368 us -> 232 us
  starting transfers between devices: 68.6 us -> 16.7 us
  local copies, waits for them, and re-layouts: 47.7 us -> 0.95 us
  Pallas kernels: 0 us -> 44.4 us
    another operation x6 -> x1, other arithmetic: 400 us -> 0.68 us  [small_inputs(): par = jnp.pad(jnp.stack([a_log, dt_bias]), ((0, 6), (0, 128 - HEADS)))]
    dot_general x161 -> x8, matrix products: 228 us -> 14.3 us  [the longest x3 13.3 us: mm(): return jnp.dot(a, b, preferred_element_type=F32)]
    ppermute x34 -> x7, waiting for transfers between devices: 199 us -> 52.9 us  [from_behind(): return lax.ppermute(block, axis, route)]
    ppermute x34 -> x7, starting transfers between devices: 68.6 us -> 16.6 us  [from_behind(): return lax.ppermute(block, axis, route)]
    pallas_call x0 -> x2, Pallas kernels: none -> 44.4 us  [the longest x1 35 us: local_pass(): pl.pallas_call(local_kernel, grid=(total // rows,), in_specs=[pl.BlockSpe...]
    mul x6 -> x0, other arithmetic: 22.9 us -> none  [the longest x1 11.4 us: block_terms(): values * strengths[..., None]]
  transfers between devices with their start and end apart: 36 -> 9, of which waited for: 33 -> 9; matrix products, arithmetic and copies ran while one was open for 39% -> 2% of each run, Pallas kernels for 0% -> 0%
where the time goes in v1:
time: 325 us; the launch traced here: 324 us
  waiting for transfers between devices  232 us (71%)
  Pallas kernels  44.4 us (14%)
  starting transfers between devices  16.7 us (5%)
  matrix products  14.3 us (4%)
  between operations  13.7 us (4%)
    reduce_scatter x1, waiting for transfers between devices, per_device(): return lax.psum_scatter(partial, 'tensor', scatter_dimension=0, tiled=True)  91 us
    all_gather x1, waiting for transfers between devices, per_device(): gathered = lax.all_gather(tokens, 'tensor', axis=0, tiled=True)  87.7 us
    ppermute x7, waiting for transfers between devices, from_behind(): return lax.ppermute(block, axis, route)  52.9 us
    pallas_call x1, Pallas kernels, local_pass(): pl.pallas_call(local_kernel, grid=(total // rows,), in_specs=[pl.BlockSpe...  35 us
    ppermute x7, starting transfers between devices, from_behind(): return lax.ppermute(block, axis, route)  16.6 us
    dot_general x3, matrix products, mm(): return jnp.dot(a, b, preferred_element_type=F32)  13.3 us
    pallas_call x1, Pallas kernels, finish(): pl.pallas_call(finish_kernel, grid=(total // rows,), in_specs=[pl.BlockSp...  9.45 us
  transfers between devices with their start and end apart: 9, of which 9 were waited for; matrix products, arithmetic and copies ran while one was open for 2% of the time, Pallas kernels for 0%

profile of v1, /device:TPU:2, one launch (start us, length us, event | category | flops | bytes accessed | tf_op | source)
XLA Modules:
  0.0 323.8 jit_solution(8820461578635160749)
XLA Ops:
  6.5 0.0 copy-start
  6.5 0.0 all-gather.2.cloned.1.call-start
  6.5 0.7 all-gather.2.cloned.1.call-update
  7.3 0.0 reduce-scatter.2.cloned.1.call-start
  7.3 0.8 copy.17
  8.1 0.7 select_maximum_fusion.par_ref
  8.8 0.7 fusion.29.taps_ref
  9.5 87.7 %all-gather.2.cloned.1.call-done = bf16[1280,2048]{1,0:T(8,128)(2,1)} async-done(((bf16[160,2048]{1,0:T(8,128)(2,1)}), bf16[1280,2048]{1,0:T(8,128)(2,1)}) %all-gather.2.cloned.1.call-update) | async-done | bytes 5242896 | tf_op jit(solution)/shard_map/all_gather | solution.py:259
  97.2 0.0 copy-start.3
  97.2 8.9 %fusion.9.pre_ref = bf16[1280,1024]{1,0:T(8,128)(2,1)S(1)} fusion(bf16[1280,2048]{1,0:T(8,128)(2,1)} %all-gather.2.cloned.1.call-done, bf16[2048,512]{1,0:T(8,128)(2,1)} %param.16, bf16[2048,256]{1,0:T(8,128)(2,1)} %param.15, bf16[2048,256]{1,0:T(8,128)(2,1)} %param.14), kind=kOutput, calls=%fused_computation.7 | convolution fusion | flops 5382602752 | bytes 12058624 | tf_op jit(solution)/shard_map/dot_general | solution.py:25
  106.1 0.0 copy-start.4
  106.1 1.9 collective-permute-start
  108.1 0.0 copy-done.3
  108.1 1.5 fusion.12.gates_ref
  109.6 0.0 copy-done.4
  109.6 0.0 copy-start.5
  109.6 3.9 %collective-permute-done.tail_ref = bf16[16,1024]{1,0:T(8,128)(2,1)S(1)} collective-permute-done((bf16[16,1024]{1,0:T(8,128)(2,1)S(1)}, bf16[16,1024]{1,0:T(8,128)(2,1)S(1)}, u32[]{:S(2)}, u32[]{:S(2)}) %collective-permute-start) | collective-permute-done | bytes 32800 | tf_op jit(solution)/shard_map/ppermute | solution.py:211
  113.5 35.0 %shard_map.127 = (bf16[1280,512]{1,0:T(8,128)(2,1)S(1)}, f32[1280,512]{1,0:T(8,128)S(1)}, f32[4,128,256]{2,1,0:T(8,128)S(1)}) custom-call(bf16[1280,1024]{1,0:T(8,128)(2,1)} %copy-done.4, bf16[16,1024]{1,0:T(8,128)(2,1)S(1)} %collective-permute-done.tail_ref, bf16[1280,128]{1,0:T(8,128)(2,1)S(1)} %fusion.12.gates_ref, f32[8,1024]{1,0:T(8,128)S(1)} %fusion.29.taps_ref, ...), custom_call_target="tpu_custom_call" | custom-call | tf_op jit(solution)/shard_map/pallas_call | solution.py:144
  148.5 0.0 copy-start.1
  148.5 1.9 collective-permute-start.1
  150.4 7.9 %collective-permute-done.1 = bf16[4,128,256]{2,1,0:T(8,128)(2,1)S(1)} collective-permute-done((bf16[4,128,256]{2,1,0:T(8,128)(2,1)S(1)}, bf16[4,128,256]{2,1,0:T(8,128)(2,1)S(1)}, u32[]{:S(2)}, u32[]{:S(2)}) %collective-permute-start.1) | collective-permute-done | bytes 262176 | tf_op jit(solution)/shard_map/ppermute | solution.py:211
  158.3 1.9 collective-permute-start.2
  160.3 7.8 %collective-permute-done.2 = bf16[4,128,256]{2,1,0:T(8,128)(2,1)S(1)} collective-permute-done((bf16[4,128,256]{2,1,0:T(8,128)(2,1)S(1)}, bf16[4,128,256]{2,1,0:T(8,128)(2,1)S(1)}, u32[]{:S(2)}, u32[]{:S(2)}) %collective-permute-start.2) | collective-permute-done | bytes 262176 | tf_op jit(solution)/shard_map/ppermute | solution.py:211
  168.1 0.2 fusion.13
  168.3 1.9 collective-permute-start.3
  170.3 8.4 %collective-permute-done.3 = bf16[4,128,256]{2,1,0:T(8,128)(2,1)S(1)} collective-permute-done((bf16[4,128,256]{2,1,0:T(8,128)(2,1)S(1)}, bf16[4,128,256]{2,1,0:T(8,128)(2,1)S(1)}, u32[]{:S(2)}, u32[]{:S(2)}) %collective-permute-start.3) | collective-permute-done | bytes 262176 | tf_op jit(solution)/shard_map/ppermute | solution.py:211
  178.7 0.2 fusion.14
  178.9 1.9 collective-permute-start.4
  180.9 13.5 %collective-permute-done.4 = bf16[4,128,256]{2,1,0:T(8,128)(2,1)S(1)} collective-permute-done((bf16[4,128,256]{2,1,0:T(8,128)(2,1)S(1)}, bf16[4,128,256]{2,1,0:T(8,128)(2,1)S(1)}, u32[]{:S(2)}, u32[]{:S(2)}) %collective-permute-start.4) | collective-permute-done | bytes 262176 | tf_op jit(solution)/shard_map/ppermute | solution.py:211
  194.3 0.2 fusion.15
  194.6 5.4 %collective-permute-start.5 = (bf16[4,128,256]{2,1,0:T(8,128)(2,1)S(1)}, bf16[4,128,256]{2,1,0:T(8,128)(2,1)S(1)}, u32[]{:S(2)}, u32[]{:S(2)}) collective-permute-start(bf16[4,128,256]{2,1,0:T(8,128)(2,1)S(1)} %fusion.15), channel_id=1, source_target_pairs={{0,64},{8,72},{16,80},{24,88},{32,96},{40,104},{48,112},{56,120},{... | collective-permute-start | bytes 786440 | tf_op jit(solution)/shard_map/ppermute | solution.py:211
  200.0 0.0 copy-done.5
  200.1 9.0 %collective-permute-done.5 = bf16[4,128,256]{2,1,0:T(8,128)(2,1)S(1)} collective-permute-done((bf16[4,128,256]{2,1,0:T(8,128)(2,1)S(1)}, bf16[4,128,256]{2,1,0:T(8,128)(2,1)S(1)}, u32[]{:S(2)}, u32[]{:S(2)}) %collective-permute-start.5) | collective-permute-done | bytes 262176 | tf_op jit(solution)/shard_map/ppermute | solution.py:211
  209.0 0.2 fusion.16
  209.3 0.0 copy-start.2
  209.3 1.6 collective-permute-start.6
  210.9 0.0 copy-done
  210.9 2.9 convolution_convert_fusion.z_ref
  213.8 0.0 copy-done.1
  213.8 2.5 collective-permute-done.6
  216.3 0.2 fusion.17.state_ref
  216.5 0.0 copy-done.2
  216.5 9.5 %shard_map.128 = bf16[1280,2048]{1,0:T(8,128)(2,1)} custom-call(bf16[1280,512]{1,0:T(8,128)(2,1)S(1)} %get-tuple-element.8.op_ref, f32[1280,512]{1,0:T(8,128)} %copy-done.1, bf16[1280,512]{1,0:T(8,128)(2,1)S(1)} %convolution_convert_fusion.z_ref, f32[1,128]{1,0:T(1,128)S(1)} %bitcast_convert_fusion.gain_ref, bf16[4,128,128]{2,1,0:T(8,128)(2,1)S(1)} %fusion.17.state_ref, ...), custom_call_target="tpu_custom_call" | custom-call | tf_op jit(solution)/shard_map/pallas_call | solution.py:189
  225.9 0.0 reduce-scatter.2.cloned.1.call-update
  226.0 91.0 %reduce-scatter.2.cloned.1.call-done = bf16[160,2048]{1,0:T(8,128)(2,1)} async-done(((bf16[1280,2048]{1,0:T(8,128)(2,1)}), bf16[160,2048]{1,0:T(8,128)(2,1)}) %reduce-scatter.2.cloned.1.call-update) | async-done | bytes 655376 | tf_op jit(solution)/shard_map/reduce_scatter | solution.py:268
  (9 shorter events, 0.2 us)
Async XLA Ops:
  6.5 204.4 %copy-start = (bf16[2048,512]{1,0:T(8,128)(2,1)S(1)}, bf16[2048,512]{1,0:T(8,128)(2,1)}, u32[]{:S(2)}) copy-start(bf16[2048,512]{1,0:T(8,128)(2,1)} %param.17) | copy-start | bytes 6291460
  6.5 90.7 %all-gather.2.cloned.1.call-start = ((), (), s32[]{:S(2)}) async-start(), calls=%async_computation.1 | async-start | bytes 5898240 | tf_op jit(solution)/shard_map/all_gather | solution.py:259
  7.3 309.7 %reduce-scatter.2.cloned.1.call-start = ((), (), s32[]{:S(2)}) async-start(), calls=%async_computation.2 | async-start | bytes 5898240 | tf_op jit(solution)/shard_map/reduce_scatter | solution.py:268
  97.2 10.8 %copy-start.3 = (bf16[1280,2048]{1,0:T(8,128)(2,1)S(1)}, bf16[1280,2048]{1,0:T(8,128)(2,1)}, u32[]{:S(2)}) copy-start(bf16[1280,2048]{1,0:T(8,128)(2,1)} %all-gather.2.cloned.1.call-done) | copy-start | bytes 15728644
  106.1 3.5 %copy-start.4 = (bf16[1280,1024]{1,0:T(8,128)(2,1)}, bf16[1280,1024]{1,0:T(8,128)(2,1)S(1)}, u32[]{:S(2)}) copy-start(bf16[1280,1024]{1,0:T(8,128)(2,1)S(1)} %fusion.9.pre_ref) | copy-start | bytes 7864324
  106.1 7.3 %collective-permute-start = (bf16[16,1024]{1,0:T(8,128)(2,1)S(1)}, bf16[16,1024]{1,0:T(8,128)(2,1)S(1)}, u32[]{:S(2)}, u32[]{:S(2)}) collective-permute-start(bf16[16,1024]{1,0:T(8,128)(2,1)S(1)} %slice.45), channel_id=1, source_target_pairs={{0,8},{8,16},{16,24},{24,32},{32,40},{40,48},{48,56},{56,64},{64,7... | collective-permute-start | bytes 98312 | tf_op jit(solution)/shard_map/ppermute | solution.py:211
  109.6 90.4 %copy-start.5 = (bf16[128]{0:T(256)(128)(2,1)S(1)}, bf16[128]{0:T(256)(128)(2,1)}, u32[]{:S(2)}) copy-start(bf16[128]{0:T(256)(128)(2,1)} %param.24) | copy-start | bytes 772
  148.5 65.3 %copy-start.1 = (f32[1280,512]{1,0:T(8,128)}, f32[1280,512]{1,0:T(8,128)S(1)}, u32[]{:S(2)}) copy-start(f32[1280,512]{1,0:T(8,128)S(1)} %get-tuple-element.9.os_ref) | copy-start | bytes 7864324
  148.5 9.8 %collective-permute-start.1 = (bf16[4,128,256]{2,1,0:T(8,128)(2,1)S(1)}, bf16[4,128,256]{2,1,0:T(8,128)(2,1)S(1)}, u32[]{:S(2)}, u32[]{:S(2)}) collective-permute-start(bf16[4,128,256]{2,1,0:T(8,128)(2,1)S(1)} %convert_element_type.59), channel_id=1, source_target_pairs={{0,8},{8,16},{16,24},{24,32},{32,40},{40,48},{48,56},{56,64},{64,7... | collective-permute-start | bytes 786440 | tf_op jit(solution)/shard_map/ppermute | solution.py:211
  158.3 9.8 %collective-permute-start.2 = (bf16[4,128,256]{2,1,0:T(8,128)(2,1)S(1)}, bf16[4,128,256]{2,1,0:T(8,128)(2,1)S(1)}, u32[]{:S(2)}, u32[]{:S(2)}) collective-permute-start(bf16[4,128,256]{2,1,0:T(8,128)(2,1)S(1)} %collective-permute-done.1), channel_id=1, source_target_pairs={{0,8},{8,16},{16,24},{24,32},{32,40},{40,48},{48,56},{56,64},{64,7... | collective-permute-start | bytes 786440 | tf_op jit(solution)/shard_map/ppermute | solution.py:211
  168.3 10.4 %collective-permute-start.3 = (bf16[4,128,256]{2,1,0:T(8,128)(2,1)S(1)}, bf16[4,128,256]{2,1,0:T(8,128)(2,1)S(1)}, u32[]{:S(2)}, u32[]{:S(2)}) collective-permute-start(bf16[4,128,256]{2,1,0:T(8,128)(2,1)S(1)} %fusion.13), channel_id=1, source_target_pairs={{0,16},{8,24},{16,32},{24,40},{32,48},{40,56},{48,64},{56,72},{64,... | collective-permute-start | bytes 786440 | tf_op jit(solution)/shard_map/ppermute | solution.py:211
  178.9 15.4 %collective-permute-start.4 = (bf16[4,128,256]{2,1,0:T(8,128)(2,1)S(1)}, bf16[4,128,256]{2,1,0:T(8,128)(2,1)S(1)}, u32[]{:S(2)}, u32[]{:S(2)}) collective-permute-start(bf16[4,128,256]{2,1,0:T(8,128)(2,1)S(1)} %fusion.14), channel_id=1, source_target_pairs={{0,32},{8,40},{16,48},{24,56},{32,64},{40,72},{48,80},{56,88},{64,... | collective-permute-start | bytes 786440 | tf_op jit(solution)/shard_map/ppermute | solution.py:211
  194.6 14.5 %collective-permute-start.5 = (bf16[4,128,256]{2,1,0:T(8,128)(2,1)S(1)}, bf16[4,128,256]{2,1,0:T(8,128)(2,1)S(1)}, u32[]{:S(2)}, u32[]{:S(2)}) collective-permute-start(bf16[4,128,256]{2,1,0:T(8,128)(2,1)S(1)} %fusion.15), channel_id=1, source_target_pairs={{0,64},{8,72},{16,80},{24,88},{32,96},{40,104},{48,112},{56,120},{... | collective-permute-start | bytes 786440 | tf_op jit(solution)/shard_map/ppermute | solution.py:211
  209.3 7.2 %copy-start.2 = (bf16[512,2048]{1,0:T(8,128)(2,1)S(1)}, bf16[512,2048]{1,0:T(8,128)(2,1)}, u32[]{:S(2)}) copy-start(bf16[512,2048]{1,0:T(8,128)(2,1)} %w_ref.1) | copy-start | bytes 6291460
  209.3 7.0 %collective-permute-start.6 = (bf16[4,128,128]{2,1,0:T(8,128)(2,1)S(1)}, bf16[4,128,128]{2,1,0:T(8,128)(2,1)S(1)}, u32[]{:S(2)}, u32[]{:S(2)}) collective-permute-start(bf16[4,128,128]{2,1,0:T(8,128)(2,1)S(1)} %slice.55), channel_id=1, source_target_pairs={{0,128},{8,136},{16,144},{24,152},{32,160},{40,168},{48,176},{56,1... | collective-permute-start | bytes 393224 | tf_op jit(solution)/shard_map/ppermute | solution.py:211
Sparse Core Ops, SparseCore 0:
  9.9 87.2 all-gather.1
  226.1 90.8 reduce-scatter.1

commit v2 on v1

--- a/solution.py
+++ b/solution.py
@@ -17,6 +17,8 @@
 PER_STEP = 2
 HEADS = 4
 KEYS = 2
+ROWS = 160
+HALF = 80
 F32 = jnp.float32
 B16 = jnp.bfloat16
 
@@ -178,29 +180,274 @@
     return jnp.concatenate(parts, axis=1)
 
 
-def finish_kernel(op_ref, os_ref, z_ref, gain_ref, state_ref, w_ref, out_ref):
-    normed = finish_rows(op_ref[...], os_ref[...], z_ref[...], gain_ref[...], state_ref[...])
-    out_ref[...] = mm(normed, w_ref[...]).astype(B16)
+def neighbours():
+    me = lax.axis_index("tensor")
+    y, x = me // 2, me % 2
+    up, down, far = ((y + d) % 4 * 2 + x for d in (1, 3, 2))
+    return me, up, down, far
+
+
+def across(index):
+    return index // 2 * 2 + 1 - index % 2
+
+
+def greet(axis, partners):
+    barrier = pltpu.get_barrier_semaphore()
+    for partner in partners:
+        pl.semaphore_signal(
+            barrier, inc=1, device_id={axis: partner}, device_id_type=pl.DeviceIdType.MESH
+        )
+    pl.semaphore_wait(barrier, len(partners))
+
+
+def rows_at(index, half=None):
+    if half is None:
+        return pl.ds(pl.multiple_of(index * ROWS, 16), ROWS)
+    return pl.ds(pl.multiple_of(index * ROWS + half * HALF, 16), HALF)
+
+
+def gather_kernel(
+    tok_ref, wq_ref, wk_ref, wv_ref, wz_ref, wg_ref, pre_ref, z_ref, gates_ref,
+    held, w_pre, w_z, w_g, w_sem, send_sem, recv_sem,
+):
+    me, up, down, far = neighbours()
+    loads = [
+        pltpu.make_async_copy(src, dst, w_sem.at[i])
+        for i, (src, dst) in enumerate(
+            (
+                (wq_ref, w_pre.at[:, 0:256]),
+                (wk_ref, w_pre.at[:, 256:512]),
+                (wv_ref, w_pre.at[:, 512:1024]),
+                (wz_ref, w_z),
+                (wg_ref, w_g),
+            )
+        )
+    ]
+    for load in loads:
+        load.start()
+    greet("tensor", (up, down, across(me)))
+
+    def copy(k, slot, half, target, own=False):
+        return pltpu.make_async_remote_copy(
+            src_ref=tok_ref.at[half * HALF : half * HALF + HALF] if own else held.at[rows_at(slot, half)],
+            dst_ref=held.at[rows_at(slot, half)],
+            send_sem=send_sem.at[k],
+            recv_sem=recv_sem.at[k],
+            device_id={"tensor": target},
+            device_id_type=pl.DeviceIdType.MESH,
+        )
+
+    sent = []
+
+    def send(k, slot, half, target, own=False):
+        made = copy(k, slot, half, target, own)
+        made.start()
+        sent.append(made)
+
+    def arrived(k, slot, half):
+        copy(k, slot, half, me).wait_recv()
+
+    def project(slot, own=False):
+        source = tok_ref if own else held.at[rows_at(slot)]
+        at = rows_at(slot)
+
+        @pl.loop(0, 4)
+        def _(i):
+            cols = pl.ds(pl.multiple_of(i * 256, 256), 256)
+            pre_ref[at, cols] = mm(source[...], w_pre[:, cols]).astype(B16)
+
+        @pl.loop(0, 2)
+        def _(i):
+            cols = pl.ds(pl.multiple_of(i * 256, 256), 256)
+            z_ref[at, cols] = mm(source[...], w_z[:, cols]).astype(B16)
+
+        gates_ref[at, :] = mm(source[...], w_g[...]).astype(B16)
+
+    send(0, me, 0, up, True)
+    send(3, me, 1, down, True)
+    send(4, me, 0, across(me), True)
+    send(5, me, 1, across(me), True)
+    send(1, me, 1, up, True)
+    send(2, me, 0, down, True)
+    for load in loads:
+        load.wait()
+    project(me, True)
+    arrived(0, down, 0)
+    send(6, down, 0, up)
+    arrived(3, up, 1)
+    send(7, up, 1, down)
+    arrived(1, down, 1)
+    project(down)
+    arrived(2, up, 0)
+    project(up)
+    arrived(4, across(me), 0)
+    send(8, across(me), 0, up)
+    send(10, across(me), 0, down)
+    arrived(5, across(me), 1)
+    send(11, across(me), 1, down)
+    send(9, across(me), 1, up)
+    project(across(me))
+    arrived(6, far, 0)
+    arrived(7, far, 1)
+    project(far)
+    arrived(8, across(down), 0)
+    send(12, across(down), 0, up)
+    arrived(11, across(up), 1)
+    send(13, across(up), 1, down)
+    arrived(9, across(down), 1)
+    project(across(down))
+    arrived(10, across(up), 0)
+    project(across(up))
+    arrived(12, across(far), 0)
+    arrived(13, across(far), 1)
+    project(across(far))
+    for made in sent:
+        made.wait_send()
+
+
+def gather_project(tokens, w_query, w_key, w_value, w_gate_z, w_gates):
+    total, depth = 8 * ROWS, tokens.shape[1]
+    vmem = pl.BlockSpec(memory_space=pltpu.VMEM)
+    hbm = pl.BlockSpec(memory_space=pl.ANY)
+    return pl.pallas_call(
+        gather_kernel,
+        in_specs=[vmem] + [hbm] * 5,
+        out_specs=[vmem] * 3,
+        out_shape=[
+            jax.ShapeDtypeStruct((total, 1024), B16),
+            jax.ShapeDtypeStruct((total, 512), B16),
+            jax.ShapeDtypeStruct((total, 128), B16),
+        ],
+        scratch_shapes=[
+            pltpu.VMEM((total, depth), B16),
+            pltpu.VMEM((depth, 1024), B16),
+            pltpu.VMEM((depth, 512), B16),
+            pltpu.VMEM((depth, 128), B16),
+            pltpu.SemaphoreType.DMA((5,)),
+            pltpu.SemaphoreType.DMA((14,)),
+            pltpu.SemaphoreType.DMA((14,)),
+        ],
+        compiler_params=pltpu.CompilerParams(
+            collective_id=0, has_side_effects=True, vmem_limit_bytes=48 * 1024 * 1024
+        ),
+    )(tokens, w_query, w_key, w_value, w_gate_z, w_gates)
+
+
+def finish_kernel(
+    op_ref, os_ref, z_ref, gain_ref, state_ref, w_ref, out_ref,
+    near, via, mine, got_via, got_up, got_down, got_x, send_sem, recv_sem,
+):
+    me, up, down, far = neighbours()
+    greet("tensor", (up, down, across(me)))
+    width = out_ref.shape[1]
+
+    def share(index, g, store):
+        row = across(index) if g == 0 else index
+        at = rows_at(row)
+        normed = finish_rows(op_ref[at, :], os_ref[at, :], z_ref[at, :], gain_ref[...], state_ref)
+
+        @pl.loop(0, width // 512)
+        def _(i):
+            cols = pl.ds(pl.multiple_of(i * 512, 512), 512)
+            store[:, cols] = mm(normed, w_ref[:, cols]).astype(B16)
+
+    sent = []
+
+    def copy(k, src, dst, target):
+        return pltpu.make_async_remote_copy(
+            src_ref=src,
+            dst_ref=dst,
+            send_sem=send_sem.at[k],
+            recv_sem=recv_sem.at[k],
+            device_id={"tensor": target},
+            device_id_type=pl.DeviceIdType.MESH,
+        )
+
+    def send(k, src, dst, target):
+        made = copy(k, src, dst, target)
+        made.start()
+        sent.append(made)
+
+    def arrived(k, dst):
+        copy(k, dst, dst, me).wait_recv()
+
+    halves = (slice(0, HALF), slice(HALF, ROWS))
+
+    def send_via(g):
+        send(g * 6, via.at[g, halves[0]], got_via.at[g, halves[0]], up)
+        send(g * 6 + 1, via.at[g, halves[1]], got_via.at[g, halves[1]], down)
+
+    def send_up(g, half):
+        send(g * 6 + 2 + half, near.at[g, 0, halves[half]], got_down.at[g, halves[half]], up)
+
+    def send_down(g, half):
+        send(g * 6 + 4 + half, near.at[g, 1, halves[half]], got_up.at[g, halves[half]], down)
+
+    def relay(g):
+        for way in (0, 1):
+            arrived(g * 6 + way, got_via.at[g, halves[way]])
+            near[g, way, halves[way], :] = (
+                near[g, way, halves[way], :].astype(F32) + got_via[g, halves[way], :].astype(F32)
+            ).astype(B16)
+            (send_up, send_down)[way](g, way)
+
+    def total(g, half):
+        arrived(g * 6 + 2 + half, got_down.at[g, halves[half]])
+        arrived(g * 6 + 4 + half, got_up.at[g, halves[half]])
+        rows = halves[half]
+        return (
+            mine[g, rows, :].astype(F32) + got_down[g, rows, :].astype(F32) + got_up[g, rows, :].astype(F32)
+        )
+
+    share(far, 0, via.at[0])
+    send_via(0)
+    share(up, 0, near.at[0, 0])
+    send_up(0, 1)
+    share(down, 0, near.at[0, 1])
+    send_down(0, 0)
+    share(far, 1, via.at[1])
+    share(up, 1, near.at[1, 0])
+    share(down, 1, near.at[1, 1])
+    relay(0)
+    send_via(1)
+    send_up(1, 1)
+    send_down(1, 0)
+    share(me, 0, mine.at[0])
+    share(me, 1, mine.at[1])
+    for half in (1, 0):
+        mine[0, halves[half], :] = total(0, half).astype(B16)
+        send(12 + half, mine.at[0, halves[half]], got_x.at[halves[half]], across(me))
+    relay(1)
+    for half in (1, 0):
+        summed = total(1, half)
+        arrived(12 + half, got_x.at[halves[half]])
+        out_ref[halves[half], :] = (summed + got_x[halves[half], :].astype(F32)).astype(B16)
+    for made in sent:
+        made.wait_send()
 
 
 def finish(op, os, z, gain, state, w_out):
-    rows = 160
-    total, width = op.shape[0], w_out.shape[1]
+    width = w_out.shape[1]
+    vmem = pl.BlockSpec(memory_space=pltpu.VMEM)
+    block = (ROWS, width)
     return pl.pallas_call(
         finish_kernel,
-        grid=(total // rows,),
-        in_specs=[
-            pl.BlockSpec((rows, 512), lambda i: (i, 0)),
-            pl.BlockSpec((rows, 512), lambda i: (i, 0)),
-            pl.BlockSpec((rows, 512), lambda i: (i, 0)),
-            pl.BlockSpec((1, DV), lambda i: (0, 0)),
-            pl.BlockSpec((HEADS, DK, DV), lambda i: (0, 0, 0)),
-            pl.BlockSpec((512, width), lambda i: (0, 0)),
+        in_specs=[vmem] * 6,
+        out_specs=vmem,
+        out_shape=jax.ShapeDtypeStruct(block, B16),
+        scratch_shapes=[
+            pltpu.VMEM((2, 2) + block, B16),
+            pltpu.VMEM((2,) + block, B16),
+            pltpu.VMEM((2,) + block, B16),
+            pltpu.VMEM((2,) + block, B16),
+            pltpu.VMEM((2,) + block, B16),
+            pltpu.VMEM((2,) + block, B16),
+            pltpu.VMEM(block, B16),
+            pltpu.SemaphoreType.DMA((14,)),
+            pltpu.SemaphoreType.DMA((14,)),
         ],
-        out_specs=pl.BlockSpec((rows, width), lambda i: (i, 0)),
-        out_shape=jax.ShapeDtypeStruct((total, width), B16),
         compiler_params=pltpu.CompilerParams(
-            dimension_semantics=("arbitrary",), vmem_limit_bytes=48 * 1024 * 1024
+            collective_id=1, has_side_effects=True, vmem_limit_bytes=48 * 1024 * 1024
         ),
     )(op, os, z, gain, state, w_out)
 
@@ -256,16 +503,13 @@
     w_out,
 ):
     taps, par, gain = small_inputs(conv_query, conv_key, conv_value, a_log, dt_bias, norm_gain)
-    gathered = lax.all_gather(tokens, "tensor", axis=0, tiled=True)
-    weights = jnp.concatenate([w_query, w_key, w_value], axis=1)
-    pre = mm(gathered, weights).astype(B16)
+    pre, z, gates = gather_project(
+        tokens, w_query, w_key, w_value, w_gate_z, gate_weights(w_gates)
+    )
     tail = from_behind(pre[pre.shape[0] - 16 :], "context", 1)
-    z = mm(gathered, w_gate_z).astype(B16)
-    gates = mm(gathered, gate_weights(w_gates)).astype(B16)
     op, os, x = local_pass(pre, tail, gates, taps, par)
     state = entering_state(x)
-    partial = finish(op, os, z, gain, state, w_out)
-    return lax.psum_scatter(partial, "tensor", scatter_dimension=0, tiled=True)
+    return finish(op, os, z, gain, state, w_out)
 
 
 def solution(mesh):

time: 325 us -> 213 us (0.66)
  waiting for transfers between devices: 232 us -> 65.6 us
  Pallas kernels: 44.4 us -> 125 us
  between operations: 13.7 us -> 0.32 us
  matrix products: 14.3 us -> 1.03 us
  starting transfers between devices: 16.7 us -> 13.1 us
  local copies, waits for them, and re-layouts: 0.95 us -> 4.4 us
    reduce_scatter x1 -> x0, waiting for transfers between devices: 91 us -> none  [per_device(): return lax.psum_scatter(partial, 'tensor', scatter_dimension=0, tiled=True)]
    all_gather x1 -> x0, waiting for transfers between devices: 87.7 us -> none  [per_device(): gathered = lax.all_gather(tokens, 'tensor', axis=0, tiled=True)]
    pallas_call x1 -> x2, Pallas kernels: 9.45 us -> 90.4 us  [the longest x1 52.5 us: gather_project(): pl.pallas_call(gather_kernel, in_specs=[vmem] + [hbm] * 5, out_specs=[vme...]
    dot_general x3 -> x0, matrix products: 13.3 us -> none  [mm(): return jnp.dot(a, b, preferred_element_type=F32)]
    ppermute x7, waiting for transfers between devices: 52.9 us -> 65.6 us  [from_behind(): return lax.ppermute(block, axis, route)]
    ppermute x7, starting transfers between devices: 16.6 us -> 13.1 us  [from_behind(): return lax.ppermute(block, axis, route)]
  transfers between devices with their start and end apart: 9 -> 7, of which waited for: 9 -> 7; matrix products, arithmetic and copies ran while one was open for 2% -> 0% of each run, Pallas kernels for 0% -> 0%
where the time goes in v2:
time: 213 us; the launch traced here: 210 us
  Pallas kernels  125 us (59%)
  waiting for transfers between devices  65.6 us (31%)
  starting transfers between devices  13.1 us (6%)
  local copies, waits for them, and re-layouts  4.4 us (2%)
    ppermute x7, waiting for transfers between devices, from_behind(): return lax.ppermute(block, axis, route)  65.6 us
    pallas_call x1, Pallas kernels, gather_project(): pl.pallas_call(gather_kernel, in_specs=[vmem] + [hbm] * 5, out_specs=[vme...  52.5 us
    pallas_call x1, Pallas kernels, finish(): pl.pallas_call(finish_kernel, in_specs=[vmem] * 6, out_specs=vmem, out_sh...  37.9 us
    pallas_call x1, Pallas kernels, local_pass(): pl.pallas_call(local_kernel, grid=(total // rows,), in_specs=[pl.BlockSpe...  34.9 us
    ppermute x7, starting transfers between devices, from_behind(): return lax.ppermute(block, axis, route)  13.1 us
  transfers between devices with their start and end apart: 7, of which 7 were waited for; matrix products, arithmetic and copies ran while one was open for 0% of the time, Pallas kernels for 0%

profile of v2, /device:TPU:2, one launch (start us, length us, event | category | flops | bytes accessed | tf_op | source)
XLA Modules:
  0.0 209.8 jit_solution(2287279661109510435)
XLA Ops:
  0.0 0.0 copy-start.4
  0.0 0.0 copy-start.2
  0.0 0.9 copy.15
  0.9 0.3 copy.16
  1.2 0.1 pad.18.wg_ref
  1.3 0.0 copy-done.4
  1.3 0.1 copy-done.2
  1.4 0.0 copy-start.3
  1.4 1.2 copy-done.3
  2.7 0.0 copy-start.5
  2.7 0.0 copy-start.6
  2.7 0.0 copy-start.7
  2.7 0.0 copy-start.8
  2.7 0.0 copy-start.9
  2.7 52.5 %shard_map.127 = (bf16[1280,1024]{1,0:T(8,128)(2,1)}, bf16[1280,512]{1,0:T(8,128)(2,1)S(1)}, bf16[1280,128]{1,0:T(8,128)(2,1)S(1)}) custom-call(bf16[160,2048]{1,0:T(8,128)(2,1)S(1)} %copy-done.4, bf16[2048,256]{1,0:T(8,128)(2,1)S(1)} %copy-done.2, bf16[2048,256]{1,0:T(8,128)(2,1)S(1)} %copy-done.3, bf16[2048,512]{1,0:T(8,128)(2,1)} %wv_ref.1, ...), custom_call_target="tpu_custom_call" | custom-call | tf_op jit(solution)/shard_map/pallas_call | solution.py:312
  55.2 0.8 slice.34
  56.0 1.9 collective-permute-start
  57.9 0.0 copy-done.5
  57.9 0.0 copy-done.6
  57.9 0.0 copy-done.7
  57.9 0.0 copy-done.8
  57.9 0.0 copy-done.9
  58.0 6.5 %collective-permute-done.tail_ref = bf16[16,1024]{1,0:T(8,128)(2,1)S(1)} collective-permute-done((bf16[16,1024]{1,0:T(8,128)(2,1)S(1)}, bf16[16,1024]{1,0:T(8,128)(2,1)S(1)}, u32[]{:S(2)}, u32[]{:S(2)}) %collective-permute-start) | collective-permute-done | bytes 32800 | tf_op jit(solution)/shard_map/ppermute | solution.py:458
  64.4 34.9 %shard_map.128 = (bf16[1280,512]{1,0:T(8,128)(2,1)S(1)}, f32[1280,512]{1,0:T(8,128)S(1)}, f32[4,128,256]{2,1,0:T(8,128)S(1)}) custom-call(bf16[1280,1024]{1,0:T(8,128)(2,1)} %get-tuple-element.11.pre_ref, bf16[16,1024]{1,0:T(8,128)(2,1)S(1)} %collective-permute-done.tail_ref, bf16[1280,128]{1,0:T(8,128)(2,1)S(1)} %get-tuple-element.12.gates_ref, ...), custom_call_target="tpu_custom_call" | custom-call | tf_op jit(solution)/shard_map/pallas_call | solution.py:146
  99.4 0.0 copy-start
  99.4 1.9 collective-permute-start.1
  101.4 7.9 %collective-permute-done.1 = bf16[4,128,256]{2,1,0:T(8,128)(2,1)S(1)} collective-permute-done((bf16[4,128,256]{2,1,0:T(8,128)(2,1)S(1)}, bf16[4,128,256]{2,1,0:T(8,128)(2,1)S(1)}, u32[]{:S(2)}, u32[]{:S(2)}) %collective-permute-start.1) | collective-permute-done | bytes 262176 | tf_op jit(solution)/shard_map/ppermute | solution.py:458
  109.2 1.9 collective-permute-start.2
  111.2 0.0 copy-start.10
  111.2 7.8 %collective-permute-done.2 = bf16[4,128,256]{2,1,0:T(8,128)(2,1)S(1)} collective-permute-done((bf16[4,128,256]{2,1,0:T(8,128)(2,1)S(1)}, bf16[4,128,256]{2,1,0:T(8,128)(2,1)S(1)}, u32[]{:S(2)}, u32[]{:S(2)}) %collective-permute-start.2) | collective-permute-done | bytes 262176 | tf_op jit(solution)/shard_map/ppermute | solution.py:458
  119.0 0.2 fusion
  119.2 0.0 copy-start.1
  119.2 2.2 %collective-permute-start.3 = (bf16[4,128,256]{2,1,0:T(8,128)(2,1)S(1)}, bf16[4,128,256]{2,1,0:T(8,128)(2,1)S(1)}, u32[]{:S(2)}, u32[]{:S(2)}) collective-permute-start(bf16[4,128,256]{2,1,0:T(8,128)(2,1)S(1)} %fusion), channel_id=1, source_target_pairs={{0,16},{8,24},{16,32},{24,40},{32,48},{40,56},{48,64},{56,72},{64,... | collective-permute-start | bytes 786440 | tf_op jit(solution)/shard_map/ppermute | solution.py:458
  121.5 8.4 %collective-permute-done.3 = bf16[4,128,256]{2,1,0:T(8,128)(2,1)S(1)} collective-permute-done((bf16[4,128,256]{2,1,0:T(8,128)(2,1)S(1)}, bf16[4,128,256]{2,1,0:T(8,128)(2,1)S(1)}, u32[]{:S(2)}, u32[]{:S(2)}) %collective-permute-start.3) | collective-permute-done | bytes 262176 | tf_op jit(solution)/shard_map/ppermute | solution.py:458
  129.9 0.2 fusion.1
  130.2 1.9 collective-permute-start.4
  132.1 17.5 %collective-permute-done.4 = bf16[4,128,256]{2,1,0:T(8,128)(2,1)S(1)} collective-permute-done((bf16[4,128,256]{2,1,0:T(8,128)(2,1)S(1)}, bf16[4,128,256]{2,1,0:T(8,128)(2,1)S(1)}, u32[]{:S(2)}, u32[]{:S(2)}) %collective-permute-start.4) | collective-permute-done | bytes 262176 | tf_op jit(solution)/shard_map/ppermute | solution.py:458
  149.6 0.2 fusion.2
  149.8 1.9 collective-permute-start.5
  151.8 0.0 copy-done
  151.8 12.0 %collective-permute-done.5 = bf16[4,128,256]{2,1,0:T(8,128)(2,1)S(1)} collective-permute-done((bf16[4,128,256]{2,1,0:T(8,128)(2,1)S(1)}, bf16[4,128,256]{2,1,0:T(8,128)(2,1)S(1)}, u32[]{:S(2)}, u32[]{:S(2)}) %collective-permute-start.5) | collective-permute-done | bytes 262176 | tf_op jit(solution)/shard_map/ppermute | solution.py:458
  163.8 0.2 fusion.3
  164.1 1.3 collective-permute-start.6
  165.4 0.0 copy-done.10
  165.4 5.5 %collective-permute-done.6 = bf16[4,128,128]{2,1,0:T(8,128)(2,1)S(1)} collective-permute-done((bf16[4,128,128]{2,1,0:T(8,128)(2,1)S(1)}, bf16[4,128,128]{2,1,0:T(8,128)(2,1)S(1)}, u32[]{:S(2)}, u32[]{:S(2)}) %collective-permute-start.6) | collective-permute-done | bytes 131104 | tf_op jit(solution)/shard_map/ppermute | solution.py:458
  170.9 0.2 fusion.4.state_ref
  171.1 0.0 copy-done.1
  171.1 37.9 %shard_map.129 = bf16[160,2048]{1,0:T(8,128)(2,1)S(1)} custom-call(bf16[1280,512]{1,0:T(8,128)(2,1)S(1)} %get-tuple-element.13.op_ref, f32[1280,512]{1,0:T(8,128)} %copy-done, bf16[1280,512]{1,0:T(8,128)(2,1)S(1)} %get-tuple-element.15.z_ref, f32[1,128]{1,0:T(1,128)S(1)} %bitcast_convert_fusion.gain_ref, bf16[4,128,128]{2,1,0:T(8,128)(2,1)S(1)} %fusion.4.state_ref, ...), custom_call_target="tpu_custom_call" | custom-call | tf_op jit(solution)/shard_map/pallas_call | solution.py:433
  209.0 0.8 copy.18
  (10 shorter events, 0.2 us)
Async XLA Ops:
  0.0 1.3 copy-start.4
  0.0 1.4 copy-start.2
  1.4 1.2 copy-start.3
  2.7 55.2 %copy-start.5 = (bf16[4,512]{1,0:T(4,128)(2,1)S(1)}, bf16[4,512]{1,0:T(4,128)(2,1)}, u32[]{:S(2)}) copy-start(bf16[4,512]{1,0:T(4,128)(2,1)} %param.21) | copy-start | bytes 12292
  2.7 55.2 %copy-start.6 = (bf16[4,256]{1,0:T(4,128)(2,1)S(1)}, bf16[4,256]{1,0:T(4,128)(2,1)}, u32[]{:S(2)}) copy-start(bf16[4,256]{1,0:T(4,128)(2,1)} %param.20) | copy-start | bytes 6148
  2.7 55.2 %copy-start.7 = (bf16[4,256]{1,0:T(4,128)(2,1)S(1)}, bf16[4,256]{1,0:T(4,128)(2,1)}, u32[]{:S(2)}) copy-start(bf16[4,256]{1,0:T(4,128)(2,1)} %param.19) | copy-start | bytes 6148
  2.7 55.2 %copy-start.8 = (f32[4]{0:T(128)S(1)}, f32[4]{0:T(128)}, u32[]{:S(2)}) copy-start(f32[4]{0:T(128)} %param.23) | copy-start | bytes 52
  2.7 55.3 %copy-start.9 = (f32[4]{0:T(128)S(1)}, f32[4]{0:T(128)}, u32[]{:S(2)}) copy-start(f32[4]{0:T(128)} %param.22) | copy-start | bytes 52
  56.0 8.5 %collective-permute-start = (bf16[16,1024]{1,0:T(8,128)(2,1)S(1)}, bf16[16,1024]{1,0:T(8,128)(2,1)S(1)}, u32[]{:S(2)}, u32[]{:S(2)}) collective-permute-start(bf16[16,1024]{1,0:T(8,128)(2,1)S(1)} %slice.34), channel_id=1, source_target_pairs={{0,8},{8,16},{16,24},{24,32},{32,40},{40,48},{48,56},{56,64},{64,7... | collective-permute-start | bytes 98312 | tf_op jit(solution)/shard_map/ppermute | solution.py:458
  99.4 52.4 %copy-start = (f32[1280,512]{1,0:T(8,128)}, f32[1280,512]{1,0:T(8,128)S(1)}, u32[]{:S(2)}) copy-start(f32[1280,512]{1,0:T(8,128)S(1)} %get-tuple-element.14.os_ref) | copy-start | bytes 7864324
  99.4 9.8 %collective-permute-start.1 = (bf16[4,128,256]{2,1,0:T(8,128)(2,1)S(1)}, bf16[4,128,256]{2,1,0:T(8,128)(2,1)S(1)}, u32[]{:S(2)}, u32[]{:S(2)}) collective-permute-start(bf16[4,128,256]{2,1,0:T(8,128)(2,1)S(1)} %convert_element_type.41), channel_id=1, source_target_pairs={{0,8},{8,16},{16,24},{24,32},{32,40},{40,48},{48,56},{56,64},{64,7... | collective-permute-start | bytes 786440 | tf_op jit(solution)/shard_map/ppermute | solution.py:458
  109.2 9.8 %collective-permute-start.2 = (bf16[4,128,256]{2,1,0:T(8,128)(2,1)S(1)}, bf16[4,128,256]{2,1,0:T(8,128)(2,1)S(1)}, u32[]{:S(2)}, u32[]{:S(2)}) collective-permute-start(bf16[4,128,256]{2,1,0:T(8,128)(2,1)S(1)} %collective-permute-done.1), channel_id=1, source_target_pairs={{0,8},{8,16},{16,24},{24,32},{32,40},{40,48},{48,56},{56,64},{64,7... | collective-permute-start | bytes 786440 | tf_op jit(solution)/shard_map/ppermute | solution.py:458
  111.2 54.2 %copy-start.10 = (bf16[128]{0:T(256)(128)(2,1)S(1)}, bf16[128]{0:T(256)(128)(2,1)}, u32[]{:S(2)}) copy-start(bf16[128]{0:T(256)(128)(2,1)} %param.24) | copy-start | bytes 772
  119.2 51.9 %copy-start.1 = (bf16[512,2048]{1,0:T(8,128)(2,1)S(1)}, bf16[512,2048]{1,0:T(8,128)(2,1)}, u32[]{:S(2)}) copy-start(bf16[512,2048]{1,0:T(8,128)(2,1)} %w_ref.1) | copy-start | bytes 6291460
  119.2 10.7 %collective-permute-start.3 = (bf16[4,128,256]{2,1,0:T(8,128)(2,1)S(1)}, bf16[4,128,256]{2,1,0:T(8,128)(2,1)S(1)}, u32[]{:S(2)}, u32[]{:S(2)}) collective-permute-start(bf16[4,128,256]{2,1,0:T(8,128)(2,1)S(1)} %fusion), channel_id=1, source_target_pairs={{0,16},{8,24},{16,32},{24,40},{32,48},{40,56},{48,64},{56,72},{64,... | collective-permute-start | bytes 786440 | tf_op jit(solution)/shard_map/ppermute | solution.py:458
  130.2 19.5 %collective-permute-start.4 = (bf16[4,128,256]{2,1,0:T(8,128)(2,1)S(1)}, bf16[4,128,256]{2,1,0:T(8,128)(2,1)S(1)}, u32[]{:S(2)}, u32[]{:S(2)}) collective-permute-start(bf16[4,128,256]{2,1,0:T(8,128)(2,1)S(1)} %fusion.1), channel_id=1, source_target_pairs={{0,32},{8,40},{16,48},{24,56},{32,64},{40,72},{48,80},{56,88},{64,... | collective-permute-start | bytes 786440 | tf_op jit(solution)/shard_map/ppermute | solution.py:458
  149.8 14.0 %collective-permute-start.5 = (bf16[4,128,256]{2,1,0:T(8,128)(2,1)S(1)}, bf16[4,128,256]{2,1,0:T(8,128)(2,1)S(1)}, u32[]{:S(2)}, u32[]{:S(2)}) collective-permute-start(bf16[4,128,256]{2,1,0:T(8,128)(2,1)S(1)} %fusion.2), channel_id=1, source_target_pairs={{0,64},{8,72},{16,80},{24,88},{32,96},{40,104},{48,112},{56,120},{... | collective-permute-start | bytes 786440 | tf_op jit(solution)/shard_map/ppermute | solution.py:458
  164.1 6.9 %collective-permute-start.6 = (bf16[4,128,128]{2,1,0:T(8,128)(2,1)S(1)}, bf16[4,128,128]{2,1,0:T(8,128)(2,1)S(1)}, u32[]{:S(2)}, u32[]{:S(2)}) collective-permute-start(bf16[4,128,128]{2,1,0:T(8,128)(2,1)S(1)} %slice.54), channel_id=1, source_target_pairs={{0,128},{8,136},{16,144},{24,152},{32,160},{40,168},{48,176},{56,1... | collective-permute-start | bytes 393224 | tf_op jit(solution)/shard_map/ppermute | solution.py:458

commit v3 on v2

--- a/solution.py
+++ b/solution.py
@@ -263,44 +263,45 @@
 
         gates_ref[at, :] = mm(source[...], w_g[...]).astype(B16)
 
-    send(0, me, 0, up, True)
+    beside, beside_down, beside_up, beside_far = (across(i) for i in (me, down, up, far))
+    send(0, me, 1, up, True)
+    send(2, me, 0, down, True)
+    send(4, me, 0, beside, True)
+    send(5, me, 1, beside, True)
+    send(1, me, 0, up, True)
     send(3, me, 1, down, True)
-    send(4, me, 0, across(me), True)
-    send(5, me, 1, across(me), True)
-    send(1, me, 1, up, True)
-    send(2, me, 0, down, True)
     for load in loads:
         load.wait()
     project(me, True)
-    arrived(0, down, 0)
-    send(6, down, 0, up)
+    arrived(0, down, 1)
+    send(6, down, 1, beside)
+    arrived(2, up, 0)
+    send(7, up, 0, beside)
+    arrived(4, beside, 0)
+    send(10, beside, 0, up)
+    arrived(1, down, 0)
+    send(8, down, 0, up)
     arrived(3, up, 1)
-    send(7, up, 1, down)
-    arrived(1, down, 1)
+    send(9, up, 1, down)
+    arrived(5, beside, 1)
+    send(11, beside, 1, down)
     project(down)
-    arrived(2, up, 0)
     project(up)
-    arrived(4, across(me), 0)
-    send(8, across(me), 0, up)
-    send(10, across(me), 0, down)
-    arrived(5, across(me), 1)
-    send(11, across(me), 1, down)
-    send(9, across(me), 1, up)
-    project(across(me))
-    arrived(6, far, 0)
-    arrived(7, far, 1)
+    project(beside)
+    arrived(10, beside_down, 0)
+    send(12, beside_down, 0, up)
+    arrived(11, beside_up, 1)
+    send(13, beside_up, 1, down)
+    arrived(8, far, 0)
+    arrived(9, far, 1)
     project(far)
-    arrived(8, across(down), 0)
-    send(12, across(down), 0, up)
-    arrived(11, across(up), 1)
-    send(13, across(up), 1, down)
-    arrived(9, across(down), 1)
-    project(across(down))
-    arrived(10, across(up), 0)
-    project(across(up))
-    arrived(12, across(far), 0)
-    arrived(13, across(far), 1)
-    project(across(far))
+    arrived(6, beside_down, 1)
+    project(beside_down)
+    arrived(7, beside_up, 0)
+    project(beside_up)
+    arrived(12, beside_far, 0)
+    arrived(13, beside_far, 1)
+    project(beside_far)
     for made in sent:
         made.wait_send()
 
@@ -334,94 +335,88 @@
 
 
 def finish_kernel(
-    op_ref, os_ref, z_ref, gain_ref, state_ref, w_ref, out_ref,
-    near, via, mine, got_via, got_up, got_down, got_x, send_sem, recv_sem,
+    op_ref, os_ref, z_ref, gain_ref, state_ref, w_ref, out_ref, part, got, send_sem, recv_sem
 ):
     me, up, down, far = neighbours()
-    greet("tensor", (up, down, across(me)))
+    beside = across(me)
+    greet("tensor", (up, down, beside))
     width = out_ref.shape[1]
 
-    def share(index, g, store):
-        row = across(index) if g == 0 else index
+    def share(slot, row):
         at = rows_at(row)
         normed = finish_rows(op_ref[at, :], os_ref[at, :], z_ref[at, :], gain_ref[...], state_ref)
 
         @pl.loop(0, width // 512)
         def _(i):
             cols = pl.ds(pl.multiple_of(i * 512, 512), 512)
-            store[:, cols] = mm(normed, w_ref[:, cols]).astype(B16)
-
+            part[slot, :, cols] = mm(normed, w_ref[:, cols]).astype(B16)
+
+    halves = (slice(0, HALF), slice(HALF, ROWS))
     sent = []
 
-    def copy(k, src, dst, target):
+    def copy(k, slot, into, half, target):
         return pltpu.make_async_remote_copy(
-            src_ref=src,
-            dst_ref=dst,
+            src_ref=part.at[slot, halves[half]],
+            dst_ref=got.at[into, halves[half]],
             send_sem=send_sem.at[k],
             recv_sem=recv_sem.at[k],
             device_id={"tensor": target},
             device_id_type=pl.DeviceIdType.MESH,
         )
 
-    def send(k, src, dst, target):
-        made = copy(k, src, dst, target)
+    def send(k, slot, into, half, target):
+        made = copy(k, slot, into, half, target)
         made.start()
         sent.append(made)
 
-    def arrived(k, dst):
-        copy(k, dst, dst, me).wait_recv()
-
-    halves = (slice(0, HALF), slice(HALF, ROWS))
-
-    def send_via(g):
-        send(g * 6, via.at[g, halves[0]], got_via.at[g, halves[0]], up)
-        send(g * 6 + 1, via.at[g, halves[1]], got_via.at[g, halves[1]], down)
-
-    def send_up(g, half):
-        send(g * 6 + 2 + half, near.at[g, 0, halves[half]], got_down.at[g, halves[half]], up)
-
-    def send_down(g, half):
-        send(g * 6 + 4 + half, near.at[g, 1, halves[half]], got_up.at[g, halves[half]], down)
-
-    def relay(g):
-        for way in (0, 1):
-            arrived(g * 6 + way, got_via.at[g, halves[way]])
-            near[g, way, halves[way], :] = (
-                near[g, way, halves[way], :].astype(F32) + got_via[g, halves[way], :].astype(F32)
-            ).astype(B16)
-            (send_up, send_down)[way](g, way)
-
-    def total(g, half):
-        arrived(g * 6 + 2 + half, got_down.at[g, halves[half]])
-        arrived(g * 6 + 4 + half, got_up.at[g, halves[half]])
+    def arrived(k, into, half):
+        copy(k, 0, into, half, me).wait_recv()
+
+    def add(k, slot, into, half):
+        arrived(k, into, half)
         rows = halves[half]
-        return (
-            mine[g, rows, :].astype(F32) + got_down[g, rows, :].astype(F32) + got_up[g, rows, :].astype(F32)
-        )
-
-    share(far, 0, via.at[0])
-    send_via(0)
-    share(up, 0, near.at[0, 0])
-    send_up(0, 1)
-    share(down, 0, near.at[0, 1])
-    send_down(0, 0)
-    share(far, 1, via.at[1])
-    share(up, 1, near.at[1, 0])
-    share(down, 1, near.at[1, 1])
-    relay(0)
-    send_via(1)
-    send_up(1, 1)
-    send_down(1, 0)
-    share(me, 0, mine.at[0])
-    share(me, 1, mine.at[1])
-    for half in (1, 0):
-        mine[0, halves[half], :] = total(0, half).astype(B16)
-        send(12 + half, mine.at[0, halves[half]], got_x.at[halves[half]], across(me))
-    relay(1)
-    for half in (1, 0):
-        summed = total(1, half)
-        arrived(12 + half, got_x.at[halves[half]])
-        out_ref[halves[half], :] = (summed + got_x[halves[half], :].astype(F32)).astype(B16)
+        part[slot, rows, :] = (
+            part[slot, rows, :].astype(F32) + got[into, rows, :].astype(F32)
+        ).astype(B16)
+
+    share(0, across(far))
+    send(0, 0, 0, 0, down)
+    send(1, 0, 0, 1, up)
+    share(1, across(down))
+    send(2, 1, 1, 1, beside)
+    share(2, across(up))
+    send(3, 2, 1, 0, beside)
+    share(4, far)
+    share(3, beside)
+    add(0, 1, 0, 0)
+    send(4, 1, 2, 0, down)
+    add(1, 2, 0, 1)
+    send(5, 2, 2, 1, up)
+    share(5, down)
+    share(6, up)
+    share(7, me)
+    send(8, 4, 4, 0, down)
+    send(9, 4, 4, 1, up)
+    add(4, 3, 2, 0)
+    send(6, 3, 3, 0, beside)
+    add(5, 3, 2, 1)
+    send(7, 3, 3, 1, beside)
+    add(2, 5, 1, 1)
+    send(11, 5, 5, 1, down)
+    add(3, 6, 1, 0)
+    send(12, 6, 6, 0, up)
+    add(8, 5, 4, 0)
+    send(10, 5, 5, 0, down)
+    add(9, 6, 4, 1)
+    send(13, 6, 6, 1, up)
+    for half, ks in ((0, (6, 12, 10)), (1, (7, 11, 13))):
+        for k in ks:
+            arrived(k, {6: 3, 7: 3, 10: 5, 11: 5, 12: 6, 13: 6}[k], half)
+        rows = halves[half]
+        total = part[7, rows, :].astype(F32)
+        for into in (3, 5, 6):
+            total = total + got[into, rows, :].astype(F32)
+        out_ref[rows, :] = total.astype(B16)
     for made in sent:
         made.wait_send()
 
@@ -429,20 +424,14 @@
 def finish(op, os, z, gain, state, w_out):
     width = w_out.shape[1]
     vmem = pl.BlockSpec(memory_space=pltpu.VMEM)
-    block = (ROWS, width)
     return pl.pallas_call(
         finish_kernel,
         in_specs=[vmem] * 6,
         out_specs=vmem,
-        out_shape=jax.ShapeDtypeStruct(block, B16),
+        out_shape=jax.ShapeDtypeStruct((ROWS, width), B16),
         scratch_shapes=[
-            pltpu.VMEM((2, 2) + block, B16),
-            pltpu.VMEM((2,) + block, B16),
-            pltpu.VMEM((2,) + block, B16),
-            pltpu.VMEM((2,) + block, B16),
-            pltpu.VMEM((2,) + block, B16),
-            pltpu.VMEM((2,) + block, B16),
-            pltpu.VMEM(block, B16),
+            pltpu.VMEM((8, ROWS, width), B16),
+            pltpu.VMEM((7, ROWS, width), B16),
             pltpu.SemaphoreType.DMA((14,)),
             pltpu.SemaphoreType.DMA((14,)),
         ],
@@ -458,21 +447,135 @@
     return lax.ppermute(block, axis, route)
 
 
+def scan_kernel(
+    x_ref, state_ref, local, pair, ring, total, before, give, back, send_sem, recv_sem
+):
+    me = lax.axis_index("context")
+    core, z, half = me % 2, me // 2 % 8, me // 16
+
+    def at(new_z):
+        return (half * 8 + (new_z + 8) % 8) * 2 + core
+
+    above, below = at(z + 1), at(z - 1)
+    other_core = me + 1 - 2 * core
+    other_half = me + 16 - 32 * half
+    greet("context", (above, below, other_core, other_half))
+    mine, theirs = pl.ds(core * 2, 2), pl.ds(2 - core * 2, 2)
+
+    def copy(k, src, dst, target):
+        return pltpu.make_async_remote_copy(
+            src_ref=src,
+            dst_ref=dst,
+            send_sem=send_sem.at[k],
+            recv_sem=recv_sem.at[k],
+            device_id={"context": target},
+            device_id_type=pl.DeviceIdType.MESH,
+        )
+
+    local[...] = x_ref[...].astype(B16)
+    swap = copy(0, local.at[theirs], pair, other_core)
+    swap.start()
+    swap.wait_recv()
+    first_core = core == 0
+    firsts = []
+    sent = [swap]
+    no_add = jnp.zeros((DK, DK), F32)
+
+    def apply(second, first):
+        added = jnp.concatenate([no_add, second[:, DK:].astype(F32)], axis=1)
+        return mm(second[:, :DK], first) + added
+
+    def slot(distance, i):
+        return ring.at[(z + distance + 8) % 8, i]
+
+    def send(k, distance, i, target):
+        made = copy(k, slot(distance, i), slot(distance, i), target)
+        made.start()
+        sent.append(made)
+
+    def arrived(k, distance, i):
+        copy(k, slot(distance, i), slot(distance, i), other_core).wait_recv()
+
+    for i in range(2):
+        own, got = local[core * 2 + i].astype(F32), pair[i].astype(F32)
+        first = jnp.where(first_core, own, got).astype(B16)
+        second = jnp.where(first_core, got, own).astype(B16)
+        firsts.append(first)
+        ring[z, i] = apply(second, first).astype(B16)
+        send(1 + i, 0, i, above)
+        send(3 + i, 0, i, below)
+    for step in (1, 2, 3):
+        for i in range(2):
+            arrived(4 * step - 3 + i, -step, i)
+            arrived(4 * step - 1 + i, step, i)
+            if step < 3 or i == 0:
+                send(4 * step + 1 + i, -step, i, above)
+            if step < 3 or i == 1:
+                send(4 * step + 3 + i, step, i, below)
+    arrived(13, 4, 0)
+    arrived(16, 4, 1)
+    folded = []
+    for i in range(2):
+        start = lax.broadcasted_iota(jnp.int32, (DK, 2 * DK), 0) == lax.broadcasted_iota(
+            jnp.int32, (DK, 2 * DK), 1
+        )
+        run = start.astype(F32)
+        here = run
+        for chip in range(8):
+            here = jnp.where(z == chip, run, here)
+            run = apply(ring[chip, i], run.astype(B16))
+        folded.append(here)
+        total[i] = run[:, DK:].astype(B16)
+    onward = copy(17, total, before, other_half)
+
+    @pl.when(half == 0)
+    def _():
+        before[...] = jnp.zeros_like(before)
+        onward.start()
+        onward.wait_send()
+
+    @pl.when(half == 1)
+    def _():
+        onward.wait_recv()
+
+    for i in range(2):
+        here = folded[i]
+        entering = mm(here[:, :DK].astype(B16), before[i]) + here[:, DK:]
+        first = firsts[i]
+        later = mm(first[:, :DK], entering.astype(B16)) + first[:, DK:].astype(F32)
+        state_ref[core * 2 + i] = jnp.where(first_core, entering, later).astype(B16)
+        give[i] = jnp.where(first_core, later, entering).astype(B16)
+    swap_back = copy(18, give, back, other_core)
+    swap_back.start()
+    swap_back.wait()
+    for i in range(2):
+        state_ref[2 - core * 2 + i] = back[i]
+    for made in sent:
+        made.wait_send()
+
+
 def entering_state(x):
-    x = from_behind(x.astype(B16), "context", 1)
-    distance, count = 1, lax.axis_size("context")
-    while distance < count:
-        last = 2 * distance >= count
-        sent = x[:, :, DK:] if last else x
-        got = from_behind(sent, "context", distance)
-        moved = jnp.einsum("hij,hjk->hik", x[:, :, :DK], got, preferred_element_type=F32)
-        if last:
-            x = moved + x[:, :, DK:].astype(F32)
-        else:
-            add = jnp.concatenate([jnp.zeros_like(x[:, :, :DK]), x[:, :, DK:]], axis=2)
-            x = (moved + add.astype(F32)).astype(B16)
-        distance *= 2
-    return x.astype(B16)
+    vmem = pl.BlockSpec(memory_space=pltpu.VMEM)
+    return pl.pallas_call(
+        scan_kernel,
+        in_specs=[vmem],
+        out_specs=vmem,
+        out_shape=jax.ShapeDtypeStruct((HEADS, DK, DV), B16),
+        scratch_shapes=[
+            pltpu.VMEM((HEADS, DK, 2 * DK), B16),
+            pltpu.VMEM((2, DK, 2 * DK), B16),
+            pltpu.VMEM((8, 2, DK, 2 * DK), B16),
+            pltpu.VMEM((2, DK, DV), B16),
+            pltpu.VMEM((2, DK, DV), B16),
+            pltpu.VMEM((2, DK, DV), B16),
+            pltpu.VMEM((2, DK, DV), B16),
+            pltpu.SemaphoreType.DMA((19,)),
+            pltpu.SemaphoreType.DMA((19,)),
+        ],
+        compiler_params=pltpu.CompilerParams(
+            collective_id=2, has_side_effects=True, vmem_limit_bytes=48 * 1024 * 1024
+        ),
+    )(x)
 
 
 def gate_weights(w_gates):

time: 213 us -> 170 us (0.80); the launches traced: 210 us -> 170 us
  waiting for transfers between devices: 65.6 us -> 5.43 us
  Pallas kernels: 125 us -> 156 us
  starting transfers between devices: 13.1 us -> 2.09 us
    ppermute x7 -> x1, waiting for transfers between devices: 65.6 us -> 5.43 us  [from_behind(): return lax.ppermute(block, axis, route)]
    pallas_call x0 -> x1, Pallas kernels: none -> 27.8 us  [entering_state(): pl.pallas_call(scan_kernel, in_specs=[vmem], out_specs=vmem, out_shape=ja...]
    ppermute x7 -> x1, starting transfers between devices: 13.1 us -> 2.09 us  [from_behind(): return lax.ppermute(block, axis, route)]
    pallas_call x1, Pallas kernels: 37.9 us -> 46.3 us  [finish(): pl.pallas_call(finish_kernel, in_specs=[vmem] * 6, out_specs=vmem, out_sh...]
    pallas_call x1, Pallas kernels: 52.5 us -> 47.1 us  [gather_project(): pl.pallas_call(gather_kernel, in_specs=[vmem] + [hbm] * 5, out_specs=[vme...]
  transfers between devices with their start and end apart: 7 -> 1, of which waited for: 7 -> 1; matrix products, arithmetic and copies ran while one was open for 0% -> 0% of each run, Pallas kernels for 0% -> 0%
where the time goes in v3:
time: 170 us
  Pallas kernels  156 us (92%)
  local copies, waits for them, and re-layouts  5.92 us (3%)
  waiting for transfers between devices  5.43 us (3%)
  starting transfers between devices  2.09 us (1%)
    pallas_call x1, Pallas kernels, gather_project(): pl.pallas_call(gather_kernel, in_specs=[vmem] + [hbm] * 5, out_specs=[vme...  47.1 us
    pallas_call x1, Pallas kernels, finish(): pl.pallas_call(finish_kernel, in_specs=[vmem] * 6, out_specs=vmem, out_sh...  46.3 us
    pallas_call x1, Pallas kernels, local_pass(): pl.pallas_call(local_kernel, grid=(total // rows,), in_specs=[pl.BlockSpe...  34.9 us
    pallas_call x1, Pallas kernels, entering_state(): pl.pallas_call(scan_kernel, in_specs=[vmem], out_specs=vmem, out_shape=ja...  27.8 us
    ppermute x1, waiting for transfers between devices, from_behind(): return lax.ppermute(block, axis, route)  5.43 us
    unnamed x23, local copies, waits for them, and re-layouts  3.72 us
  transfers between devices with their start and end apart: 1, of which 1 were waited for; matrix products, arithmetic and copies ran while one was open for 0% of the time, Pallas kernels for 0%

profile of v3, /device:TPU:2, one launch (start us, length us, event | category | flops | bytes accessed | tf_op | source)
XLA Modules:
  0.0 169.8 jit_solution(4487753516176503040)
XLA Ops:
  0.0 0.0 copy-start.4
  0.0 0.0 copy-start.2
  0.0 0.9 copy.15
  0.9 0.3 copy.16
  1.2 0.1 pad.14.wg_ref
  1.3 0.0 copy-done.4
  1.3 0.1 copy-done.2
  1.4 0.0 copy-start.3
  1.4 1.2 copy-done.3
  2.7 0.0 copy-start.10
  2.7 0.0 copy-start.5
  2.7 0.0 copy-start.6
  2.7 0.0 copy-start.7
  2.7 0.0 copy-start.8
  2.7 0.0 copy-start.9
  2.7 47.1 %shard_map.127 = (bf16[1280,1024]{1,0:T(8,128)(2,1)}, bf16[1280,512]{1,0:T(8,128)(2,1)S(1)}, bf16[1280,128]{1,0:T(8,128)(2,1)S(1)}) custom-call(bf16[160,2048]{1,0:T(8,128)(2,1)S(1)} %copy-done.4, bf16[2048,256]{1,0:T(8,128)(2,1)S(1)} %copy-done.2, bf16[2048,256]{1,0:T(8,128)(2,1)S(1)} %copy-done.3, bf16[2048,512]{1,0:T(8,128)(2,1)} %wv_ref.1, ...), custom_call_target="tpu_custom_call" | custom-call | tf_op jit(solution)/shard_map/pallas_call | solution.py:313
  49.8 0.0 copy-start.1
  49.8 0.9 slice.3
  50.7 2.1 %collective-permute-start = (bf16[16,1024]{1,0:T(8,128)(2,1)S(1)}, bf16[16,1024]{1,0:T(8,128)(2,1)S(1)}, u32[]{:S(2)}, u32[]{:S(2)}) collective-permute-start(bf16[16,1024]{1,0:T(8,128)(2,1)S(1)} %slice.3), channel_id=1, source_target_pairs={{0,8},{8,16},{16,24},{24,32},{32,40},{40,48},{48,56},{56,64},{64,7... | collective-permute-start | bytes 98312 | tf_op jit(solution)/shard_map/ppermute | solution.py:447
  52.8 0.0 copy-done.10
  52.8 0.0 copy-done.5
  52.9 0.0 copy-done.6
  52.9 0.0 copy-done.7
  52.9 0.0 copy-done.8
  52.9 0.0 copy-done.9
  52.9 5.4 %collective-permute-done.tail_ref = bf16[16,1024]{1,0:T(8,128)(2,1)S(1)} collective-permute-done((bf16[16,1024]{1,0:T(8,128)(2,1)S(1)}, bf16[16,1024]{1,0:T(8,128)(2,1)S(1)}, u32[]{:S(2)}, u32[]{:S(2)}) %collective-permute-start) | collective-permute-done | bytes 32800 | tf_op jit(solution)/shard_map/ppermute | solution.py:447
  58.4 34.9 %shard_map.128 = (bf16[1280,512]{1,0:T(8,128)(2,1)S(1)}, f32[1280,512]{1,0:T(8,128)S(1)}, f32[4,128,256]{2,1,0:T(8,128)S(1)}) custom-call(bf16[1280,1024]{1,0:T(8,128)(2,1)} %get-tuple-element.11.pre_ref, bf16[16,1024]{1,0:T(8,128)(2,1)S(1)} %collective-permute-done.tail_ref, bf16[1280,128]{1,0:T(8,128)(2,1)S(1)} %get-tuple-element.12.gates_ref, ...), custom_call_target="tpu_custom_call" | custom-call | tf_op jit(solution)/shard_map/pallas_call | solution.py:146
  93.3 0.0 copy-start
  93.3 1.5 copy-done
  94.8 27.8 %shard_map.129.state_ref = bf16[4,128,128]{2,1,0:T(8,128)(2,1)S(1)} custom-call(f32[4,128,256]{2,1,0:T(8,128)S(1)} %get-tuple-element.16.x_ref), custom_call_target="tpu_custom_call" | custom-call | tf_op jit(solution)/shard_map/pallas_call | solution.py:559
  122.6 0.0 copy-done.1
  122.6 46.3 %shard_map.130 = bf16[160,2048]{1,0:T(8,128)(2,1)S(1)} custom-call(bf16[1280,512]{1,0:T(8,128)(2,1)S(1)} %get-tuple-element.13.op_ref, f32[1280,512]{1,0:T(8,128)} %copy-done, bf16[1280,512]{1,0:T(8,128)(2,1)S(1)} %get-tuple-element.15.z_ref, f32[1,128]{1,0:T(1,128)S(1)} %bitcast_convert_fusion.gain_ref, bf16[4,128,128]{2,1,0:T(8,128)(2,1)S(1)} %shard_map.129.state_ref, ...), custom_call_target="tpu_custom_call" | custom-call | tf_op jit(solution)/shard_map/pallas_call | solution.py:427
  168.9 0.8 copy.18
  (4 shorter events, 0.0 us)
Async XLA Ops:
  0.0 1.3 copy-start.4
  0.0 1.4 copy-start.2
  1.4 1.2 copy-start.3
  2.7 50.2 %copy-start.10 = (bf16[128]{0:T(256)(128)(2,1)S(1)}, bf16[128]{0:T(256)(128)(2,1)}, u32[]{:S(2)}) copy-start(bf16[128]{0:T(256)(128)(2,1)} %param.24) | copy-start | bytes 772
  2.7 50.2 %copy-start.5 = (bf16[4,512]{1,0:T(4,128)(2,1)S(1)}, bf16[4,512]{1,0:T(4,128)(2,1)}, u32[]{:S(2)}) copy-start(bf16[4,512]{1,0:T(4,128)(2,1)} %param.21) | copy-start | bytes 12292
  2.7 50.2 %copy-start.6 = (bf16[4,256]{1,0:T(4,128)(2,1)S(1)}, bf16[4,256]{1,0:T(4,128)(2,1)}, u32[]{:S(2)}) copy-start(bf16[4,256]{1,0:T(4,128)(2,1)} %param.20) | copy-start | bytes 6148
  2.7 50.2 %copy-start.7 = (bf16[4,256]{1,0:T(4,128)(2,1)S(1)}, bf16[4,256]{1,0:T(4,128)(2,1)}, u32[]{:S(2)}) copy-start(bf16[4,256]{1,0:T(4,128)(2,1)} %param.19) | copy-start | bytes 6148
  2.7 50.2 %copy-start.8 = (f32[4]{0:T(128)S(1)}, f32[4]{0:T(128)}, u32[]{:S(2)}) copy-start(f32[4]{0:T(128)} %param.23) | copy-start | bytes 52
  2.7 50.2 %copy-start.9 = (f32[4]{0:T(128)S(1)}, f32[4]{0:T(128)}, u32[]{:S(2)}) copy-start(f32[4]{0:T(128)} %param.22) | copy-start | bytes 52
  49.8 72.8 %copy-start.1 = (bf16[512,2048]{1,0:T(8,128)(2,1)S(1)}, bf16[512,2048]{1,0:T(8,128)(2,1)}, u32[]{:S(2)}) copy-start(bf16[512,2048]{1,0:T(8,128)(2,1)} %w_ref.1) | copy-start | bytes 6291460
  50.7 7.6 %collective-permute-start = (bf16[16,1024]{1,0:T(8,128)(2,1)S(1)}, bf16[16,1024]{1,0:T(8,128)(2,1)S(1)}, u32[]{:S(2)}, u32[]{:S(2)}) collective-permute-start(bf16[16,1024]{1,0:T(8,128)(2,1)S(1)} %slice.3), channel_id=1, source_target_pairs={{0,8},{8,16},{16,24},{24,32},{32,40},{40,48},{48,56},{56,64},{64,7... | collective-permute-start | bytes 98312 | tf_op jit(solution)/shard_map/ppermute | solution.py:447
  93.3 1.5 copy-start

commit v4 on v3

--- a/solution.py
+++ b/solution.py
@@ -14,7 +14,8 @@
 KW = 4
 EPSILON = 1e-06
 LEN = 128
-PER_STEP = 2
+PER_STEP = 5
+SOLVE = 64
 HEADS = 4
 KEYS = 2
 ROWS = 160
@@ -43,54 +44,74 @@
     return x * lax.rsqrt(jnp.sum(x * x, axis=-1, keepdims=True) + EPSILON)
 
 
-def chunk_terms(q_all, k_all, v_all, gates, gate_par):
+def chunk_terms(convs, gates, gate_par):
     ii = lax.broadcasted_iota(jnp.int32, (LEN, LEN), 0)
     jj = lax.broadcasted_iota(jnp.int32, (LEN, LEN), 1)
     lower = (ii >= jj).astype(F32)
     strict = (ii > jj).astype(F32)
     differ = ii ^ jj
-    levels = [((differ >> s) == 1).astype(B16) for s in range(LEN.bit_length() - 1)]
+    levels = [((differ >> s) == 1).astype(B16) for s in range(SOLVE.bit_length() - 1)]
     eye = (ii == jj).astype(B16)
 
-    logits = gates.astype(F32)
-    shifted = logits + gate_par[1:2, :]
-    softplus = jnp.maximum(shifted, 0.0) + jnp.log1p(jnp.exp(-jnp.abs(shifted)))
-    decays = -jnp.exp(gate_par[0:1, :]) * softplus
-    beta = 1.0 / (1.0 + jnp.exp(-logits))
-    cum = jnp.dot(lower, decays, preferred_element_type=F32, precision=lax.Precision.HIGHEST)
-    cum_t = cum.T
-    growth = jnp.exp(cum)
-    fade = jnp.exp(cum[LEN - 1 : LEN, :] - cum)
+    units = []
+    for conv in convs:
+        for g in range(KEYS):
+            qf = unit(conv[:, g * DK : (g + 1) * DK]) * (DK**-0.5)
+            kf = unit(conv[:, 256 + g * DK : 256 + (g + 1) * DK])
+            units.append((qf, kf, qf.astype(B16), kf.astype(B16)))
+    kks = [mm_nt(kb, kb) * strict for _, _, _, kb in units]
+    qks = [mm_nt(qb, kb) * lower for _, _, qb, kb in units]
+
+    logits = [gate.astype(F32) for gate in gates]
+    shifted = [x + gate_par[1:2, :] for x in logits]
+    softplus = [jnp.maximum(x, 0.0) + jnp.log1p(jnp.exp(-jnp.abs(x))) for x in shifted]
+    rate = -jnp.exp(gate_par[0:1, :])
+    cums = [
+        jnp.dot(lower, rate * x, preferred_element_type=F32, precision=lax.Precision.HIGHEST)
+        for x in softplus
+    ]
 
     terms = []
-    for g in range(KEYS):
-        qf = unit(q_all[:, g * DK : (g + 1) * DK]) * (DK**-0.5)
-        kf = unit(k_all[:, g * DK : (g + 1) * DK])
-        qb, kb = qf.astype(B16), kf.astype(B16)
-        kk = mm_nt(kb, kb) * strict
-        qk = mm_nt(qb, kb) * lower
-        for h in (2 * g, 2 * g + 1):
+    for c, (conv, cum) in enumerate(zip(convs, cums)):
+        beta = 1.0 / (1.0 + jnp.exp(-logits[c]))
+        cum_t = cum.T
+        growth = jnp.exp(cum)
+        fade = jnp.exp(cum[LEN - 1 : LEN, :] - cum)
+        for h in range(HEADS):
+            qf, kf, _, _ = units[c * KEYS + h // 2]
+            kk, qk = kks[c * KEYS + h // 2], qks[c * KEYS + h // 2]
             spread = jnp.exp(jnp.minimum(cum[:, h : h + 1] - cum_t[h : h + 1, :], 0.0))
             b = beta[:, 4 + h : 5 + h]
             a = (kk * spread * b).astype(B16)
             r = (qk * spread).astype(B16)
-            vb = (v_all[:, h * DV : (h + 1) * DV] * b).astype(B16)
+            vb = (conv[:, 512 + h * DV : 512 + (h + 1) * DV] * b).astype(B16)
             grow = growth[:, h : h + 1]
             src = jnp.concatenate([(kf * (b * grow)).astype(B16), vb], axis=1)
             fk = (kf * fade[:, h : h + 1]).astype(B16)
-            terms.append([a, r, src, fk, qf * grow, growth[LEN - 1 : LEN, h : h + 1]])
+            terms.append((a, r, src, fk, qf * grow, growth[LEN - 1 : LEN, h : h + 1]))
     inv = [eye - t[0] * levels[0] for t in terms]
     for level in levels[1:]:
         part = [mm(t[0] * level, x).astype(B16) for t, x in zip(terms, inv)]
         inv = [x - mm(x, p).astype(B16) for x, p in zip(inv, part)]
-    out = []
-    for (a, r, src, fk, qg, last), x in zip(terms, inv):
-        yw = mm(x, src).astype(B16)
-        ryw = mm(r, yw)
-        fyw = mm_tn(fk, yw)
-        q_new = (qg - ryw[:, :DK]).astype(B16)
-        out.append((q_new, ryw[:, DK:], fyw[:, :DK].astype(B16), fyw[:, DK:], last))
-    return out
+    found = [[] for _ in terms]
+    for i in range(LEN // SOLVE):
+        rows = slice(i * SOLVE, (i + 1) * SOLVE)
+        rhs = [t[2][rows] for t in terms]
+        if i:
+            known = [jnp.concatenate(f, axis=0) if i > 1 else f[0] for f in found]
+            rhs = [
+                (x.astype(F32) - mm(t[0][rows, : i * SOLVE], k)).astype(B16)
+                for t, x, k in zip(terms, rhs, known)
+            ]
+        for f, x, y in zip(found, inv, rhs):
+            f.append(mm(x[rows, rows], y).astype(B16))
+    yws = [jnp.concatenate(f, axis=0) for f in found]
+    fyws = [mm_tn(t[3], yw) for t, yw in zip(terms, yws)]
+    ryws = [mm(t[1], yw) for t, yw in zip(terms, yws)]
+    return [
+        ((t[4] - ryw[:, :DK]).astype(B16), ryw[:, DK:], fyw[:, :DK].astype(B16), fyw[:, DK:], t[5])
+        for t, ryw, fyw in zip(terms, ryws, fyws)
+    ]
 
 
 def local_kernel(pre_ref, tail_ref, gates_ref, taps_ref, par_ref, op_ref, os_ref, x_ref, ext):
@@ -113,31 +134,30 @@
     ext[8 : rows + 8, :] = pre_ref[...].astype(F32)
     taps = taps_ref[...]
     par = par_ref[...]
-    done = []
+    convs = []
     for c in range(PER_STEP):
         base = c * LEN + 8
         conv = taps[0:1, :] * ext[base - 3 : base - 3 + LEN, :]
         for j in range(1, KW):
             conv = conv + taps[j : j + 1, :] * ext[base - 3 + j : base - 3 + j + LEN, :]
-        conv = silu(conv)
-        done.append(
-            chunk_terms(
-                conv[:, :256], conv[:, 256:512], conv[:, 512:], gates_ref[c * LEN : (c + 1) * LEN, :], par
-            )
-        )
+        convs.append(silu(conv))
+    gates = [gates_ref[c * LEN : (c + 1) * LEN, :] for c in range(PER_STEP)]
+    done = chunk_terms(convs, gates, par)
+    xs = [x_ref[h] for h in range(HEADS)]
+    for c in range(PER_STEP):
+        at = slice(c * LEN, (c + 1) * LEN)
+        now = done[c * HEADS : (c + 1) * HEADS]
+        xbs = [x.astype(B16) for x in xs]
+        moved = [mm(d[2], xb) for d, xb in zip(now, xbs)]
+        seen = [mm(d[0], xb) for d, xb in zip(now, xbs)]
+        for h in range(HEADS):
+            cols = slice(h * DV, (h + 1) * DV)
+            op_ref[at, cols] = seen[h][:, :DK].astype(B16)
+            os_ref[at, cols] = seen[h][:, DK:] + now[h][1]
+            x = xs[h] * now[h][4] - moved[h]
+            xs[h] = jnp.concatenate([x[:, :DK], x[:, DK:] + now[h][3]], axis=1)
     for h in range(HEADS):
-        x = x_ref[h]
-        for c in range(PER_STEP):
-            q_new, own, move, add, last = done[c][h]
-            xb = x.astype(B16)
-            seen = mm(q_new, xb)
-            at = slice(c * LEN, (c + 1) * LEN)
-            cols = slice(h * DV, (h + 1) * DV)
-            op_ref[at, cols] = seen[:, :DK].astype(B16)
-            os_ref[at, cols] = seen[:, DK:] + own
-            x = x * last - mm(move, xb)
-            x = jnp.concatenate([x[:, :DK], x[:, DK:] + add], axis=1)
-        x_ref[h] = x
+        x_ref[h] = xs[h]
 
 
 def local_pass(pre, tail, gates, taps, par):
@@ -191,11 +211,12 @@
     return index // 2 * 2 + 1 - index % 2
 
 
-def greet(axis, partners):
+def greet(partners):
     barrier = pltpu.get_barrier_semaphore()
+    partners = tuple(partners)
     for partner in partners:
         pl.semaphore_signal(
-            barrier, inc=1, device_id={axis: partner}, device_id_type=pl.DeviceIdType.MESH
+            barrier, inc=1, device_id=partner, device_id_type=pl.DeviceIdType.MESH
         )
     pl.semaphore_wait(barrier, len(partners))
 
@@ -207,8 +228,8 @@
 
 
 def gather_kernel(
-    tok_ref, wq_ref, wk_ref, wv_ref, wz_ref, wg_ref, pre_ref, z_ref, gates_ref,
-    held, w_pre, w_z, w_g, w_sem, send_sem, recv_sem,
+    tok_ref, wq_ref, wk_ref, wv_ref, wz_ref, wg_ref, pre_ref, z_ref, gates_ref, tail_ref,
+    held, got_tail, w_pre, w_z, w_g, w_sem, send_sem, recv_sem,
 ):
     me, up, down, far = neighbours()
     loads = [
@@ -225,7 +246,20 @@
     ]
     for load in loads:
         load.start()
-    greet("tensor", (up, down, across(me)))
+    context = lax.axis_index("context")
+    after = (context + 1) % 32
+    greet(
+        [{"tensor": i} for i in (up, down, across(me))]
+        + [{"context": i} for i in (after, (context + 31) % 32)]
+    )
+    tail_copy = pltpu.make_async_remote_copy(
+        src_ref=pre_ref.at[8 * ROWS - 16 : 8 * ROWS],
+        dst_ref=got_tail,
+        send_sem=send_sem.at[14],
+        recv_sem=recv_sem.at[14],
+        device_id={"context": after},
+        device_id_type=pl.DeviceIdType.MESH,
+    )
 
     def copy(k, slot, half, target, own=False):
         return pltpu.make_async_remote_copy(
@@ -262,6 +296,10 @@
             z_ref[at, cols] = mm(source[...], w_z[:, cols]).astype(B16)
 
         gates_ref[at, :] = mm(source[...], w_g[...]).astype(B16)
+
+        @pl.when(slot == 7)
+        def _():
+            tail_copy.start()
 
     beside, beside_down, beside_up, beside_far = (across(i) for i in (me, down, up, far))
     send(0, me, 1, up, True)
@@ -302,6 +340,14 @@
     arrived(12, beside_far, 0)
     arrived(13, beside_far, 1)
     project(beside_far)
+    tail_copy.wait_recv()
+    tail_ref[...] = got_tail[...]
+
+    @pl.when(context == 0)
+    def _():
+        tail_ref[...] = jnp.zeros_like(tail_ref)
+
+    tail_copy.wait_send()
     for made in sent:
         made.wait_send()
 
@@ -313,20 +359,22 @@
     return pl.pallas_call(
         gather_kernel,
         in_specs=[vmem] + [hbm] * 5,
-        out_specs=[vmem] * 3,
+        out_specs=[vmem] * 4,
         out_shape=[
             jax.ShapeDtypeStruct((total, 1024), B16),
             jax.ShapeDtypeStruct((total, 512), B16),
             jax.ShapeDtypeStruct((total, 128), B16),
+            jax.ShapeDtypeStruct((16, 1024), B16),
         ],
         scratch_shapes=[
             pltpu.VMEM((total, depth), B16),
+            pltpu.VMEM((16, 1024), B16),
             pltpu.VMEM((depth, 1024), B16),
             pltpu.VMEM((depth, 512), B16),
             pltpu.VMEM((depth, 128), B16),
             pltpu.SemaphoreType.DMA((5,)),
-            pltpu.SemaphoreType.DMA((14,)),
-            pltpu.SemaphoreType.DMA((14,)),
+            pltpu.SemaphoreType.DMA((15,)),
+            pltpu.SemaphoreType.DMA((15,)),
         ],
         compiler_params=pltpu.CompilerParams(
             collective_id=0, has_side_effects=True, vmem_limit_bytes=48 * 1024 * 1024
@@ -339,7 +387,7 @@
 ):
     me, up, down, far = neighbours()
     beside = across(me)
-    greet("tensor", (up, down, beside))
+    greet({"tensor": i} for i in (up, down, beside))
     width = out_ref.shape[1]
 
     def share(slot, row):
@@ -441,12 +489,6 @@
     )(op, os, z, gain, state, w_out)
 
 
-def from_behind(block, axis, distance):
-    devices = range(lax.axis_size(axis))
-    route = [(i - distance, i) for i in devices if i - distance in devices]
-    return lax.ppermute(block, axis, route)
-
-
 def scan_kernel(
     x_ref, state_ref, local, pair, ring, total, before, give, back, send_sem, recv_sem
 ):
@@ -459,7 +501,7 @@
     above, below = at(z + 1), at(z - 1)
     other_core = me + 1 - 2 * core
     other_half = me + 16 - 32 * half
-    greet("context", (above, below, other_core, other_half))
+    greet({"context": i} for i in (above, below, other_core, other_half))
     mine, theirs = pl.ds(core * 2, 2), pl.ds(2 - core * 2, 2)
 
     def copy(k, src, dst, target):
@@ -606,10 +648,9 @@
     w_out,
 ):
     taps, par, gain = small_inputs(conv_query, conv_key, conv_value, a_log, dt_bias, norm_gain)
-    pre, z, gates = gather_project(
+    pre, z, gates, tail = gather_project(
         tokens, w_query, w_key, w_value, w_gate_z, gate_weights(w_gates)
     )
-    tail = from_behind(pre[pre.shape[0] - 16 :], "context", 1)
     op, os, x = local_pass(pre, tail, gates, taps, par)
     state = entering_state(x)
     return finish(op, os, z, gain, state, w_out)

time: 170 us -> 148 us (0.87)
  Pallas kernels: 156 us -> 142 us
  waiting for transfers between devices: 5.43 us -> 0 us
  starting transfers between devices: 2.09 us -> 0 us
    pallas_call x1, Pallas kernels: 34.9 us -> 17.7 us  [local_pass(): pl.pallas_call(local_kernel, grid=(total // rows,), in_specs=[pl.BlockSpe...]
    ppermute x1 -> x0, waiting for transfers between devices: 5.43 us -> none  [from_behind(): return lax.ppermute(block, axis, route)]
    pallas_call x1, Pallas kernels: 47.1 us -> 50 us  [gather_project(): pl.pallas_call(gather_kernel, in_specs=[vmem] + [hbm] * 5, out_specs=[vme...]
    ppermute x1 -> x0, starting transfers between devices: 2.09 us -> none  [from_behind(): return lax.ppermute(block, axis, route)]
  transfers between devices with their start and end apart: 1 -> 0, of which waited for: 1 -> 0; matrix products, arithmetic and copies ran while one was open for 0% -> 0% of each run, Pallas kernels for 0% -> 0%
where the time goes in v4:
time: 148 us; the launch traced here: 147 us
  Pallas kernels  142 us (96%)
  local copies, waits for them, and re-layouts  5.01 us (3%)
    pallas_call x1, Pallas kernels, gather_project(): pl.pallas_call(gather_kernel, in_specs=[vmem] + [hbm] * 5, out_specs=[vme...  50 us
    pallas_call x1, Pallas kernels, finish(): pl.pallas_call(finish_kernel, in_specs=[vmem] * 6, out_specs=vmem, out_sh...  47.3 us
    pallas_call x1, Pallas kernels, entering_state(): pl.pallas_call(scan_kernel, in_specs=[vmem], out_specs=vmem, out_shape=ja...  27.2 us
    pallas_call x1, Pallas kernels, local_pass(): pl.pallas_call(local_kernel, grid=(total // rows,), in_specs=[pl.BlockSpe...  17.7 us
    unnamed x23, local copies, waits for them, and re-layouts  3.72 us

profile of v4, /device:TPU:2, one launch (start us, length us, event | category | flops | bytes accessed | tf_op | source)
XLA Modules:
  0.0 147.4 jit_solution(3343428501049195221)
XLA Ops:
  0.0 0.0 copy-start.4
  0.0 0.0 copy-start.2
  0.0 0.9 copy.15
  0.9 0.3 copy.16
  1.2 0.1 pad.14.wg_ref
  1.3 0.0 copy-done.4
  1.3 0.1 copy-done.2
  1.4 0.0 copy-start.3
  1.4 1.2 copy-done.3
  2.7 0.0 copy-start.5
  2.7 0.0 copy-start.6
  2.7 0.0 copy-start.7
  2.7 0.0 copy-start.8
  2.7 0.0 copy-start.9
  2.7 50.0 %shard_map.127 = (bf16[1280,1024]{1,0:T(8,128)(2,1)}, bf16[1280,512]{1,0:T(8,128)(2,1)S(1)}, bf16[1280,128]{1,0:T(8,128)(2,1)S(1)}, bf16[16,1024]{1,0:T(8,128)(2,1)S(1)}) custom-call(bf16[160,2048]{1,0:T(8,128)(2,1)S(1)} %copy-done.4, bf16[2048,256]{1,0:T(8,128)(2,1)S(1)} %copy-done.2, bf16[2048,256]{1,0:T(8,128)(2,1)S(1)} %copy-done.3, ...), custom_call_target="tpu_custom_call" | custom-call | tf_op jit(solution)/shard_map/pallas_call | solution.py:359
  52.7 0.0 copy-start.10
  52.7 0.0 copy-start.1
  52.8 0.0 copy-done.5
  52.8 0.0 copy-done.6
  52.8 0.0 copy-done.7
  52.8 0.0 copy-done.8
  52.8 0.0 copy-done.9
  52.8 17.7 %shard_map.128 = (bf16[1280,512]{1,0:T(8,128)(2,1)S(1)}, f32[1280,512]{1,0:T(8,128)S(1)}, f32[4,128,256]{2,1,0:T(8,128)S(1)}) custom-call(bf16[1280,1024]{1,0:T(8,128)(2,1)} %get-tuple-element.12.pre_ref, bf16[16,1024]{1,0:T(8,128)(2,1)S(1)} %get-tuple-element.13.tail_ref, bf16[1280,128]{1,0:T(8,128)(2,1)S(1)} %get-tuple-element.14.gates_ref, ...), custom_call_target="tpu_custom_call" | custom-call | tf_op jit(solution)/shard_map/pallas_call | solution.py:166
  70.5 0.0 copy-start
  70.5 1.5 %copy-done = f32[1280,512]{1,0:T(8,128)} copy-done((f32[1280,512]{1,0:T(8,128)}, f32[1280,512]{1,0:T(8,128)S(1)}, u32[]{:S(2)}) %copy-start) | copy-done | bytes 2621464
  72.0 27.2 %shard_map.129.state_ref = bf16[4,128,128]{2,1,0:T(8,128)(2,1)S(1)} custom-call(f32[4,128,256]{2,1,0:T(8,128)S(1)} %get-tuple-element.18.x_ref), custom_call_target="tpu_custom_call" | custom-call | tf_op jit(solution)/shard_map/pallas_call | solution.py:601
  99.3 0.0 copy-done.10
  99.3 0.0 copy-done.1
  99.3 47.3 %shard_map.130 = bf16[160,2048]{1,0:T(8,128)(2,1)S(1)} custom-call(bf16[1280,512]{1,0:T(8,128)(2,1)S(1)} %get-tuple-element.15.op_ref, f32[1280,512]{1,0:T(8,128)} %copy-done, bf16[1280,512]{1,0:T(8,128)(2,1)S(1)} %get-tuple-element.17.z_ref, f32[1,128]{1,0:T(1,128)S(1)} %bitcast_convert_fusion.gain_ref, bf16[4,128,128]{2,1,0:T(8,128)(2,1)S(1)} %shard_map.129.state_ref, ...), custom_call_target="tpu_custom_call" | custom-call | tf_op jit(solution)/shard_map/pallas_call | solution.py:475
  146.6 0.8 copy.18
  (4 shorter events, 0.0 us)
Async XLA Ops:
  0.0 1.3 copy-start.4
  0.0 1.4 copy-start.2
  1.4 1.2 copy-start.3
  2.7 50.1 %copy-start.5 = (bf16[4,512]{1,0:T(4,128)(2,1)S(1)}, bf16[4,512]{1,0:T(4,128)(2,1)}, u32[]{:S(2)}) copy-start(bf16[4,512]{1,0:T(4,128)(2,1)} %param.21) | copy-start | bytes 12292
  2.7 50.1 %copy-start.6 = (bf16[4,256]{1,0:T(4,128)(2,1)S(1)}, bf16[4,256]{1,0:T(4,128)(2,1)}, u32[]{:S(2)}) copy-start(bf16[4,256]{1,0:T(4,128)(2,1)} %param.20) | copy-start | bytes 6148
  2.7 50.1 %copy-start.7 = (bf16[4,256]{1,0:T(4,128)(2,1)S(1)}, bf16[4,256]{1,0:T(4,128)(2,1)}, u32[]{:S(2)}) copy-start(bf16[4,256]{1,0:T(4,128)(2,1)} %param.19) | copy-start | bytes 6148
  2.7 50.1 %copy-start.8 = (f32[4]{0:T(128)S(1)}, f32[4]{0:T(128)}, u32[]{:S(2)}) copy-start(f32[4]{0:T(128)} %param.23) | copy-start | bytes 52
  2.7 50.1 %copy-start.9 = (f32[4]{0:T(128)S(1)}, f32[4]{0:T(128)}, u32[]{:S(2)}) copy-start(f32[4]{0:T(128)} %param.22) | copy-start | bytes 52
  52.7 46.5 %copy-start.10 = (bf16[128]{0:T(256)(128)(2,1)S(1)}, bf16[128]{0:T(256)(128)(2,1)}, u32[]{:S(2)}) copy-start(bf16[128]{0:T(256)(128)(2,1)} %param.24) | copy-start | bytes 772
  52.7 46.5 %copy-start.1 = (bf16[512,2048]{1,0:T(8,128)(2,1)S(1)}, bf16[512,2048]{1,0:T(8,128)(2,1)}, u32[]{:S(2)}) copy-start(bf16[512,2048]{1,0:T(8,128)(2,1)} %w_ref.1) | copy-start | bytes 6291460
  70.5 1.5 %copy-start = (f32[1280,512]{1,0:T(8,128)}, f32[1280,512]{1,0:T(8,128)S(1)}, u32[]{:S(2)}) copy-start(f32[1280,512]{1,0:T(8,128)S(1)} %get-tuple-element.16.os_ref) | copy-start | bytes 7864324

commit v5 on v4

--- a/solution.py
+++ b/solution.py
@@ -218,7 +218,7 @@
         pl.semaphore_signal(
             barrier, inc=1, device_id=partner, device_id_type=pl.DeviceIdType.MESH
         )
-    pl.semaphore_wait(barrier, len(partners))
+    return lambda: pl.semaphore_wait(barrier, len(partners))
 
 
 def rows_at(index, half=None):
@@ -244,14 +244,15 @@
             )
         )
     ]
-    for load in loads:
-        load.start()
     context = lax.axis_index("context")
     after = (context + 1) % 32
-    greet(
+    all_here = greet(
         [{"tensor": i} for i in (up, down, across(me))]
         + [{"context": i} for i in (after, (context + 31) % 32)]
     )
+    for load in loads:
+        load.start()
+    all_here()
     tail_copy = pltpu.make_async_remote_copy(
         src_ref=pre_ref.at[8 * ROWS - 16 : 8 * ROWS],
         dst_ref=got_tail,
@@ -387,7 +388,7 @@
 ):
     me, up, down, far = neighbours()
     beside = across(me)
-    greet({"tensor": i} for i in (up, down, beside))
+    all_here = greet({"tensor": i} for i in (up, down, beside))
     width = out_ref.shape[1]
 
     def share(slot, row):
@@ -428,6 +429,7 @@
         ).astype(B16)
 
     share(0, across(far))
+    all_here()
     send(0, 0, 0, 0, down)
     send(1, 0, 0, 1, up)
     share(1, across(down))
@@ -484,7 +486,7 @@
             pltpu.SemaphoreType.DMA((14,)),
         ],
         compiler_params=pltpu.CompilerParams(
-            collective_id=1, has_side_effects=True, vmem_limit_bytes=48 * 1024 * 1024
+            collective_id=1, has_side_effects=True, vmem_limit_bytes=28 * 1024 * 1024
         ),
     )(op, os, z, gain, state, w_out)
 
@@ -501,7 +503,7 @@
     above, below = at(z + 1), at(z - 1)
     other_core = me + 1 - 2 * core
     other_half = me + 16 - 32 * half
-    greet({"context": i} for i in (above, below, other_core, other_half))
+    all_here = greet({"context": i} for i in (above, below, other_core, other_half))
     mine, theirs = pl.ds(core * 2, 2), pl.ds(2 - core * 2, 2)
 
     def copy(k, src, dst, target):
@@ -515,6 +517,7 @@
         )
 
     local[...] = x_ref[...].astype(B16)
+    all_here()
     swap = copy(0, local.at[theirs], pair, other_core)
     swap.start()
     swap.wait_recv()
@@ -615,7 +618,7 @@
             pltpu.SemaphoreType.DMA((19,)),
         ],
         compiler_params=pltpu.CompilerParams(
-            collective_id=2, has_side_effects=True, vmem_limit_bytes=48 * 1024 * 1024
+            collective_id=2, has_side_effects=True, vmem_limit_bytes=8 * 1024 * 1024
         ),
     )(x)
 

time: 148 us -> 143 us (0.966)
  Pallas kernels: 142 us -> 139 us
  local copies, waits for them, and re-layouts: 5.01 us -> 3.51 us
    pallas_call x1, Pallas kernels: 47.3 us -> 44.2 us  [finish(): pl.pallas_call(finish_kernel, in_specs=[vmem] * 6, out_specs=vmem, out_sh...]
    unnamed x23 -> x21, local copies, waits for them, and re-layouts: 3.72 us -> 2.22 us
where the time goes in v5:
time: 143 us
  Pallas kernels  139 us (97%)
  local copies, waits for them, and re-layouts  3.51 us (2%)
    pallas_call x1, Pallas kernels, gather_project(): pl.pallas_call(gather_kernel, in_specs=[vmem] + [hbm] * 5, out_specs=[vme...  49.7 us
    pallas_call x1, Pallas kernels, finish(): pl.pallas_call(finish_kernel, in_specs=[vmem] * 6, out_specs=vmem, out_sh...  44.2 us
    pallas_call x1, Pallas kernels, entering_state(): pl.pallas_call(scan_kernel, in_specs=[vmem], out_specs=vmem, out_shape=ja...  27.4 us
    pallas_call x1, Pallas kernels, local_pass(): pl.pallas_call(local_kernel, grid=(total // rows,), in_specs=[pl.BlockSpe...  17.7 us

profile of v5, /device:TPU:2, one launch (start us, length us, event | category | flops | bytes accessed | tf_op | source)
XLA Modules:
  0.0 142.7 jit_solution(17871916450370869450)
XLA Ops:
  0.0 0.0 copy-start.3
  0.0 0.0 copy-start.1
  0.0 0.9 copy.15
  0.9 0.3 copy.16
  1.2 0.1 pad.14.wg_ref
  1.3 0.0 copy-done.3
  1.3 0.1 copy-done.1
  1.4 0.0 copy-start.2
  1.4 1.2 copy-done.2
  2.7 0.0 copy-start.4
  2.7 0.0 copy-start.5
  2.7 0.0 copy-start.6
  2.7 0.0 copy-start.7
  2.7 0.0 copy-start.8
  2.7 49.7 %shard_map.127 = (bf16[1280,1024]{1,0:T(8,128)(2,1)}, bf16[1280,512]{1,0:T(8,128)(2,1)S(1)}, bf16[1280,128]{1,0:T(8,128)(2,1)S(1)}, bf16[16,1024]{1,0:T(8,128)(2,1)S(1)}) custom-call(bf16[160,2048]{1,0:T(8,128)(2,1)S(1)} %copy-done.3, bf16[2048,256]{1,0:T(8,128)(2,1)S(1)} %copy-done.1, bf16[2048,256]{1,0:T(8,128)(2,1)S(1)} %copy-done.2, ...), custom_call_target="tpu_custom_call" | custom-call | tf_op jit(solution)/shard_map/pallas_call | solution.py:360
  52.4 0.0 copy-start.9
  52.4 0.0 copy-start
  52.4 0.0 copy-done.4
  52.4 0.0 copy-done.5
  52.4 0.0 copy-done.6
  52.5 0.0 copy-done.7
  52.5 0.0 copy-done.8
  52.5 17.7 %shard_map.128 = (bf16[1280,512]{1,0:T(8,128)(2,1)S(1)}, f32[1280,512]{1,0:T(8,128)S(1)}, f32[4,128,256]{2,1,0:T(8,128)S(1)}) custom-call(bf16[1280,1024]{1,0:T(8,128)(2,1)} %get-tuple-element.12.pre_ref, bf16[16,1024]{1,0:T(8,128)(2,1)S(1)} %get-tuple-element.13.tail_ref, bf16[1280,128]{1,0:T(8,128)(2,1)S(1)} %get-tuple-element.14.gates_ref, ...), custom_call_target="tpu_custom_call" | custom-call | tf_op jit(solution)/shard_map/pallas_call | solution.py:166
  70.2 27.4 %shard_map.129.state_ref = bf16[4,128,128]{2,1,0:T(8,128)(2,1)S(1)} custom-call(f32[4,128,256]{2,1,0:T(8,128)S(1)} %get-tuple-element.18.x_ref), custom_call_target="tpu_custom_call" | custom-call | tf_op jit(solution)/shard_map/pallas_call | solution.py:604
  97.5 0.0 copy-done.9
  97.6 0.0 copy-done
  97.6 44.2 %shard_map.130 = bf16[160,2048]{1,0:T(8,128)(2,1)S(1)} custom-call(bf16[1280,512]{1,0:T(8,128)(2,1)S(1)} %get-tuple-element.15.op_ref, f32[1280,512]{1,0:T(8,128)S(1)} %get-tuple-element.16.os_ref, bf16[1280,512]{1,0:T(8,128)(2,1)S(1)} %get-tuple-element.17.z_ref, f32[1,128]{1,0:T(1,128)S(1)} %bitcast_convert_fusion.gain_ref, ...), custom_call_target="tpu_custom_call" | custom-call | tf_op jit(solution)/shard_map/pallas_call | solution.py:477
  141.8 0.8 copy.18
  (4 shorter events, 0.0 us)
Async XLA Ops:
  0.0 1.3 copy-start.3
  0.0 1.4 %copy-start.1 = (bf16[2048,256]{1,0:T(8,128)(2,1)S(1)}, bf16[2048,256]{1,0:T(8,128)(2,1)}, u32[]{:S(2)}) copy-start(bf16[2048,256]{1,0:T(8,128)(2,1)} %wq_ref.1) | copy-start | bytes 3145732
  1.4 1.2 copy-start.2
  2.7 49.8 %copy-start.4 = (bf16[4,512]{1,0:T(4,128)(2,1)S(1)}, bf16[4,512]{1,0:T(4,128)(2,1)}, u32[]{:S(2)}) copy-start(bf16[4,512]{1,0:T(4,128)(2,1)} %param.21) | copy-start | bytes 12292
  2.7 49.8 %copy-start.5 = (bf16[4,256]{1,0:T(4,128)(2,1)S(1)}, bf16[4,256]{1,0:T(4,128)(2,1)}, u32[]{:S(2)}) copy-start(bf16[4,256]{1,0:T(4,128)(2,1)} %param.20) | copy-start | bytes 6148
  2.7 49.8 %copy-start.6 = (bf16[4,256]{1,0:T(4,128)(2,1)S(1)}, bf16[4,256]{1,0:T(4,128)(2,1)}, u32[]{:S(2)}) copy-start(bf16[4,256]{1,0:T(4,128)(2,1)} %param.19) | copy-start | bytes 6148
  2.7 49.8 %copy-start.7 = (f32[4]{0:T(128)S(1)}, f32[4]{0:T(128)}, u32[]{:S(2)}) copy-start(f32[4]{0:T(128)} %param.23) | copy-start | bytes 52
  2.7 49.8 %copy-start.8 = (f32[4]{0:T(128)S(1)}, f32[4]{0:T(128)}, u32[]{:S(2)}) copy-start(f32[4]{0:T(128)} %param.22) | copy-start | bytes 52
  52.4 45.1 %copy-start.9 = (bf16[128]{0:T(256)(128)(2,1)S(1)}, bf16[128]{0:T(256)(128)(2,1)}, u32[]{:S(2)}) copy-start(bf16[128]{0:T(256)(128)(2,1)} %param.24) | copy-start | bytes 772
  52.4 45.2 %copy-start = (bf16[512,2048]{1,0:T(8,128)(2,1)S(1)}, bf16[512,2048]{1,0:T(8,128)(2,1)}, u32[]{:S(2)}) copy-start(bf16[512,2048]{1,0:T(8,128)(2,1)} %w_ref.1) | copy-start | bytes 6291460

commit v6 on v5

--- a/solution.py
+++ b/solution.py
@@ -192,9 +192,9 @@
 
 def finish_rows(seen, own, z, gain, state):
     parts = []
-    for h in range(HEADS):
-        cols = slice(h * DV, (h + 1) * DV)
-        core = mm(seen[:, cols], state[h]) + own[:, cols]
+    heads = [slice(h * DV, (h + 1) * DV) for h in range(HEADS)]
+    cores = [mm(seen[:, cols], state[h]) + own[:, cols] for h, cols in enumerate(heads)]
+    for core, cols in zip(cores, heads):
         scale = lax.rsqrt(jnp.mean(core * core, axis=-1, keepdims=True) + EPSILON)
         parts.append((core * scale * gain * silu(z[:, cols].astype(F32))).astype(B16))
     return jnp.concatenate(parts, axis=1)
@@ -559,18 +559,16 @@
                 send(4 * step + 3 + i, step, i, below)
     arrived(13, 4, 0)
     arrived(16, 4, 1)
-    folded = []
+    start = lax.broadcasted_iota(jnp.int32, (DK, 2 * DK), 0) == lax.broadcasted_iota(
+        jnp.int32, (DK, 2 * DK), 1
+    )
+    runs = [start.astype(F32)] * 2
+    folded = runs
+    for chip in range(8):
+        folded = [jnp.where(z == chip, run, here) for run, here in zip(runs, folded)]
+        runs = [apply(ring[chip, i], runs[i].astype(B16)) for i in range(2)]
     for i in range(2):
-        start = lax.broadcasted_iota(jnp.int32, (DK, 2 * DK), 0) == lax.broadcasted_iota(
-            jnp.int32, (DK, 2 * DK), 1
-        )
-        run = start.astype(F32)
-        here = run
-        for chip in range(8):
-            here = jnp.where(z == chip, run, here)
-            run = apply(ring[chip, i], run.astype(B16))
-        folded.append(here)
-        total[i] = run[:, DK:].astype(B16)
+        total[i] = runs[i][:, DK:].astype(B16)
     onward = copy(17, total, before, other_half)
 
     @pl.when(half == 0)
@@ -583,13 +581,14 @@
     def _():
         onward.wait_recv()
 
+    entering = [mm(x[:, :DK].astype(B16), before[i]) + x[:, DK:] for i, x in enumerate(folded)]
+    later = [
+        mm(first[:, :DK], x.astype(B16)) + first[:, DK:].astype(F32)
+        for first, x in zip(firsts, entering)
+    ]
     for i in range(2):
-        here = folded[i]
-        entering = mm(here[:, :DK].astype(B16), before[i]) + here[:, DK:]
-        first = firsts[i]
-        later = mm(first[:, :DK], entering.astype(B16)) + first[:, DK:].astype(F32)
-        state_ref[core * 2 + i] = jnp.where(first_core, entering, later).astype(B16)
-        give[i] = jnp.where(first_core, later, entering).astype(B16)
+        state_ref[core * 2 + i] = jnp.where(first_core, entering[i], later[i]).astype(B16)
+        give[i] = jnp.where(first_core, later[i], entering[i]).astype(B16)
     swap_back = copy(18, give, back, other_core)
     swap_back.start()
     swap_back.wait()

time: 143 us -> 142 us (level)
  no operation moved by 1% of the time
where the time goes in v6:
time: 142 us
  Pallas kernels  138 us (97%)
  local copies, waits for them, and re-layouts  3.51 us (2%)
    pallas_call x1, Pallas kernels, gather_project(): pl.pallas_call(gather_kernel, in_specs=[vmem] + [hbm] * 5, out_specs=[vme...  49.7 us
    pallas_call x1, Pallas kernels, finish(): pl.pallas_call(finish_kernel, in_specs=[vmem] * 6, out_specs=vmem, out_sh...  44.2 us
    pallas_call x1, Pallas kernels, entering_state(): pl.pallas_call(scan_kernel, in_specs=[vmem], out_specs=vmem, out_shape=ja...  26.5 us
    pallas_call x1, Pallas kernels, local_pass(): pl.pallas_call(local_kernel, grid=(total // rows,), in_specs=[pl.BlockSpe...  17.7 us

profile of v6, /device:TPU:2, one launch (start us, length us, event | category | flops | bytes accessed | tf_op | source)
XLA Modules:
  0.0 141.8 jit_solution(12938921306139158863)
XLA Ops:
  0.0 0.0 copy-start.3
  0.0 0.0 copy-start.1
  0.0 0.9 copy.15
  0.9 0.3 copy.16
  1.2 0.1 pad.14.wg_ref
  1.3 0.0 copy-done.3
  1.3 0.1 copy-done.1
  1.4 0.0 copy-start.2
  1.4 1.2 copy-done.2
  2.7 0.0 copy-start.4
  2.7 0.0 copy-start.5
  2.7 0.0 copy-start.6
  2.7 0.0 copy-start.7
  2.7 0.0 copy-start.8
  2.7 49.7 %shard_map.127 = (bf16[1280,1024]{1,0:T(8,128)(2,1)}, bf16[1280,512]{1,0:T(8,128)(2,1)S(1)}, bf16[1280,128]{1,0:T(8,128)(2,1)S(1)}, bf16[16,1024]{1,0:T(8,128)(2,1)S(1)}) custom-call(bf16[160,2048]{1,0:T(8,128)(2,1)S(1)} %copy-done.3, bf16[2048,256]{1,0:T(8,128)(2,1)S(1)} %copy-done.1, bf16[2048,256]{1,0:T(8,128)(2,1)S(1)} %copy-done.2, ...), custom_call_target="tpu_custom_call" | custom-call | tf_op jit(solution)/shard_map/pallas_call | solution.py:360
  52.4 0.0 copy-start.9
  52.4 0.0 copy-start
  52.4 0.0 copy-done.4
  52.4 0.0 copy-done.5
  52.4 0.0 copy-done.6
  52.5 0.0 copy-done.7
  52.5 0.0 copy-done.8
  52.5 17.7 %shard_map.128 = (bf16[1280,512]{1,0:T(8,128)(2,1)S(1)}, f32[1280,512]{1,0:T(8,128)S(1)}, f32[4,128,256]{2,1,0:T(8,128)S(1)}) custom-call(bf16[1280,1024]{1,0:T(8,128)(2,1)} %get-tuple-element.12.pre_ref, bf16[16,1024]{1,0:T(8,128)(2,1)S(1)} %get-tuple-element.13.tail_ref, bf16[1280,128]{1,0:T(8,128)(2,1)S(1)} %get-tuple-element.14.gates_ref, ...), custom_call_target="tpu_custom_call" | custom-call | tf_op jit(solution)/shard_map/pallas_call | solution.py:166
  70.2 26.5 %shard_map.129.state_ref = bf16[4,128,128]{2,1,0:T(8,128)(2,1)S(1)} custom-call(f32[4,128,256]{2,1,0:T(8,128)S(1)} %get-tuple-element.18.x_ref), custom_call_target="tpu_custom_call" | custom-call | tf_op jit(solution)/shard_map/pallas_call | solution.py:603
  96.7 0.0 copy-done.9
  96.7 0.0 copy-done
  96.7 44.2 %shard_map.130 = bf16[160,2048]{1,0:T(8,128)(2,1)S(1)} custom-call(bf16[1280,512]{1,0:T(8,128)(2,1)S(1)} %get-tuple-element.15.op_ref, f32[1280,512]{1,0:T(8,128)S(1)} %get-tuple-element.16.os_ref, bf16[1280,512]{1,0:T(8,128)(2,1)S(1)} %get-tuple-element.17.z_ref, f32[1,128]{1,0:T(1,128)S(1)} %bitcast_convert_fusion.gain_ref, ...), custom_call_target="tpu_custom_call" | custom-call | tf_op jit(solution)/shard_map/pallas_call | solution.py:477
  141.0 0.8 copy.18
  (4 shorter events, 0.0 us)
Async XLA Ops:
  0.0 1.3 copy-start.3
  0.0 1.4 %copy-start.1 = (bf16[2048,256]{1,0:T(8,128)(2,1)S(1)}, bf16[2048,256]{1,0:T(8,128)(2,1)}, u32[]{:S(2)}) copy-start(bf16[2048,256]{1,0:T(8,128)(2,1)} %wq_ref.1) | copy-start | bytes 3145732
  1.4 1.2 copy-start.2
  2.7 49.8 %copy-start.4 = (bf16[4,512]{1,0:T(4,128)(2,1)S(1)}, bf16[4,512]{1,0:T(4,128)(2,1)}, u32[]{:S(2)}) copy-start(bf16[4,512]{1,0:T(4,128)(2,1)} %param.21) | copy-start | bytes 12292
  2.7 49.8 %copy-start.5 = (bf16[4,256]{1,0:T(4,128)(2,1)S(1)}, bf16[4,256]{1,0:T(4,128)(2,1)}, u32[]{:S(2)}) copy-start(bf16[4,256]{1,0:T(4,128)(2,1)} %param.20) | copy-start | bytes 6148
  2.7 49.8 %copy-start.6 = (bf16[4,256]{1,0:T(4,128)(2,1)S(1)}, bf16[4,256]{1,0:T(4,128)(2,1)}, u32[]{:S(2)}) copy-start(bf16[4,256]{1,0:T(4,128)(2,1)} %param.19) | copy-start | bytes 6148
  2.7 49.8 %copy-start.7 = (f32[4]{0:T(128)S(1)}, f32[4]{0:T(128)}, u32[]{:S(2)}) copy-start(f32[4]{0:T(128)} %param.23) | copy-start | bytes 52
  2.7 49.8 %copy-start.8 = (f32[4]{0:T(128)S(1)}, f32[4]{0:T(128)}, u32[]{:S(2)}) copy-start(f32[4]{0:T(128)} %param.22) | copy-start | bytes 52
  52.4 44.3 %copy-start.9 = (bf16[128]{0:T(256)(128)(2,1)S(1)}, bf16[128]{0:T(256)(128)(2,1)}, u32[]{:S(2)}) copy-start(bf16[128]{0:T(256)(128)(2,1)} %param.24) | copy-start | bytes 772
  52.4 44.3 %copy-start = (bf16[512,2048]{1,0:T(8,128)(2,1)S(1)}, bf16[512,2048]{1,0:T(8,128)(2,1)}, u32[]{:S(2)}) copy-start(bf16[512,2048]{1,0:T(8,128)(2,1)} %w_ref.1) | copy-start | bytes 6291460
